TPU v7x, 32 devices: a whole 2x2x4 slice. The times are simulated.
32 devices in a mesh: segment: 2 (over core), expert: 4 (over z), pair: 4 (over y, x).
Axes of the slice: x: 2, y: 2, z: 4, core: 2. Of those that a mesh axis runs over, the one named last changes fastest.
Arguments:
- acts: bfloat16 [2, 2, 768, 768], P(None, None, 'expert', 'pair'), may hold values from -20 to 20
- cotangent: bfloat16 [2, 768, 768], P(None, 'expert', 'pair'), may hold values from -6 to 6
- gates: float32 [2, 2, 768], P(None, None, 'expert'), may hold values from 0.2 to 1
- owners: int32 [2, 2, 768], P(None, None, 'expert'), may hold values from 0 to 3, as said below
- slots: int32 [2, 2, 768], P(None, None, 'expert'), may hold values from 0 to 59
- w_in: bfloat16 [2, 4, 768, 3072], P('segment', 'expert', None, 'pair'), may hold values from -0.21875 to 0.21875
- w_out: bfloat16 [2, 4, 3072, 768], P('segment', 'expert', 'pair'), may hold values from -0.109375 to 0.109375
Outputs:
- grads: bfloat16 [2, 2, 768, 768], P('segment', None, 'expert', 'pair')
- grad_in: bfloat16 [2, 4, 768, 3072], P('segment', 'expert', None, 'pair')
- grad_out: bfloat16 [2, 4, 3072, 768], P('segment', 'expert', 'pair')
Inputs may be any that keep to these rules, and one draw needn't show every extreme that they name: `owners`: within each aligned block of 192 tokens of one sublayer and micro-batch, no two tokens share both owner and slot. One expert, the same for all blocks of a draw, takes exactly 60 tokens of every block.
All inputs are finite; a program needn't handle non-finite values.
Results may differ from a plain program's by a relative error of at most 0.02.
Values may be sent and summed in bfloat16 or wider, within the bound.
A program may use at most 64 MiB of HBM per device.

v0:
```python
import jax
import jax.numpy as jnp
from jax import lax
from jax.sharding import PartitionSpec as P


def from_behind(x, axis, by):
    count = lax.axis_size(axis)
    pairs = [(i, i + by) for i in range(count) if 0 <= i + by < count]
    return lax.ppermute(x, axis, pairs)


def gelu_value(pre_act):
    inner_arg = 0.7978845608 * (pre_act + 0.044715 * pre_act * pre_act * pre_act)
    return 0.5 * pre_act * (1.0 + jnp.tanh(inner_arg))


def gelu_slope(pre_act):
    inner_arg = 0.7978845608 * (pre_act + 0.044715 * pre_act * pre_act * pre_act)
    tangent = jnp.tanh(inner_arg)
    return 0.5 * (1.0 + tangent) + 0.5 * pre_act * (1.0 - tangent * tangent) * 0.7978845608 * (
        1.0 + 0.134145 * pre_act * pre_act
    )


def layer_pass(
    token_acts, upstream, gate_row, owner_row, slot_row, first_weights, second_weights, capacity
):
    tok_rows, feat_share = token_acts.shape
    expert_count = lax.axis_size("expert")
    pair_count = lax.axis_size("pair")
    width = feat_share * pair_count
    slot_rows = expert_count * capacity
    scaled = (gate_row[:, None] * upstream.astype(jnp.float32)).astype(jnp.bfloat16)
    target = owner_row * capacity + slot_row
    placing = (lax.broadcasted_iota(jnp.int32, (slot_rows, tok_rows), 0) == target[None, :]).astype(
        jnp.bfloat16
    )
    joined = jnp.concatenate([token_acts, scaled], axis=1)
    packed = jnp.dot(placing, joined, preferred_element_type=jnp.float32).astype(jnp.bfloat16)
    arrived = lax.all_to_all(
        packed.reshape(expert_count, capacity, 2 * feat_share),
        "expert",
        split_axis=0,
        concat_axis=0,
        tiled=True,
    )
    gathered = lax.all_gather(arrived.reshape(slot_rows, 2, feat_share), "pair", axis=2, tiled=True)
    slot_acts = gathered[:, 0]
    slot_grad = gathered[:, 1]
    act_float = slot_acts.astype(jnp.float32)
    scale_inv = lax.rsqrt(jnp.mean(act_float * act_float, axis=1) + 1e-06)
    normed = (act_float * scale_inv[:, None]).astype(jnp.bfloat16)
    pre_act = jnp.dot(normed, first_weights, preferred_element_type=jnp.float32)
    hidden = gelu_value(pre_act).astype(jnp.bfloat16)
    back_hidden = lax.dot_general(
        slot_grad, second_weights, (((1,), (1,)), ((), ())), preferred_element_type=jnp.float32
    )
    back_pre = (back_hidden * gelu_slope(pre_act)).astype(jnp.bfloat16)
    grad_first = lax.dot_general(
        normed, back_pre, (((0,), (0,)), ((), ())), preferred_element_type=jnp.float32
    )
    grad_second = lax.dot_general(
        hidden, slot_grad, (((0,), (0,)), ((), ())), preferred_element_type=jnp.float32
    )
    contract = (((1,), (1,)), ((), ()))
    half = first_weights.shape[1] // 2
    lower_part = lax.dot_general(
        back_pre[:, :half], first_weights[:, :half], contract, preferred_element_type=jnp.float32
    ).astype(jnp.bfloat16)
    upper_part = lax.dot_general(
        back_pre[:, half:], first_weights[:, half:], contract, preferred_element_type=jnp.float32
    ).astype(jnp.bfloat16)
    lower_part, upper_part = lax.optimization_barrier((lower_part, upper_part))
    partial_value = lower_part.astype(jnp.float32) + upper_part.astype(jnp.float32)
    summed = lax.psum(partial_value.astype(jnp.bfloat16), "pair").astype(jnp.float32)
    own_start = lax.axis_index("pair") * feat_share
    own_acts = lax.dynamic_slice_in_dim(act_float, own_start, feat_share, 1)
    inner = jnp.sum(summed * act_float, axis=1)
    own_sum = lax.dynamic_slice_in_dim(summed, own_start, feat_share, 1)
    branch = (
        scale_inv[:, None] * own_sum - (scale_inv**3 * inner / width)[:, None] * own_acts
    ).astype(jnp.bfloat16)
    returned = lax.all_to_all(
        branch.reshape(expert_count, capacity, feat_share),
        "expert",
        split_axis=0,
        concat_axis=0,
        tiled=True,
    )
    restored = lax.dot_general(
        placing,
        returned.reshape(slot_rows, feat_share),
        (((0,), (0,)), ((), ())),
        preferred_element_type=jnp.float32,
    )
    result = (upstream.astype(jnp.float32) + restored).astype(jnp.bfloat16)
    return (result, grad_first, grad_second)


def body(acts, cotangent, gates, owners, slots, w_in, w_out):
    segment_index = lax.axis_index("segment")
    micro_count = acts.shape[1]
    tok_rows = acts.shape[2]
    feat_share = acts.shape[3]
    expert_count = lax.axis_size("expert")
    capacity = max(2, (5 * tok_rows + 4 * expert_count - 1) // (4 * expert_count))
    own_first = w_in[0, 0]
    own_second = w_out[0, 0]
    layer_acts = lax.dynamic_index_in_dim(acts, segment_index, 0, False)
    layer_gates = lax.dynamic_index_in_dim(gates, segment_index, 0, False)
    layer_owners = lax.dynamic_index_in_dim(owners, segment_index, 0, False)
    layer_slots = lax.dynamic_index_in_dim(slots, segment_index, 0, False)
    first_total = jnp.zeros(own_first.shape, jnp.float32)
    second_total = jnp.zeros(own_second.shape, jnp.float32)
    results = jnp.zeros((micro_count, tok_rows, feat_share), jnp.bfloat16)
    received = jnp.zeros((tok_rows, feat_share), jnp.bfloat16)
    for tick in range(micro_count + 1):
        current = tick - 1 + segment_index
        usable = (current >= 0) & (current < micro_count)
        chosen = jnp.clip(current, 0, micro_count - 1)
        token_acts = lax.dynamic_index_in_dim(layer_acts, chosen, 0, False)
        gate_row = lax.dynamic_index_in_dim(layer_gates, chosen, 0, False)
        owner_row = lax.dynamic_index_in_dim(layer_owners, chosen, 0, False)
        slot_row = lax.dynamic_index_in_dim(layer_slots, chosen, 0, False)
        upstream = jnp.where(segment_index == 1, cotangent[min(tick, micro_count - 1)], received)
        result, grad_first, grad_second = layer_pass(
            token_acts, upstream, gate_row, owner_row, slot_row, own_first, own_second, capacity
        )
        weight_mask = usable.astype(jnp.float32)
        first_total = first_total + weight_mask * grad_first
        second_total = second_total + weight_mask * grad_second
        results = jnp.where(
            usable, lax.dynamic_update_index_in_dim(results, result, chosen, 0), results
        )
        if tick < micro_count:
            received = from_behind(result, "segment", -1)
    return (
        results[None],
        first_total.astype(jnp.bfloat16)[None, None],
        second_total.astype(jnp.bfloat16)[None, None],
    )


def solution(mesh):
    placed = (
        P(None, None, "expert", "pair"),
        P(None, "expert", "pair"),
        P(None, None, "expert"),
        P(None, None, "expert"),
        P(None, None, "expert"),
        P("segment", "expert", None, "pair"),
        P("segment", "expert", "pair", None),
    )
    return jax.shard_map(
        body,
        mesh=mesh,
        in_specs=placed,
        out_specs=(
            P("segment", None, "expert", "pair"),
            P("segment", "expert", None, "pair"),
            P("segment", "expert", "pair", None),
        ),
        check_vma=False,
    )
```

profile of v0, /device:TPU:0, one launch (start us, length us, event | category | flops | bytes accessed | tf_op | source)
XLA Modules:
  0.0 316.0 jit_solution(11158699666871983308)
XLA Ops:
  8.1 1.7 dynamic-slice_bitcast_fusion
  11.9 13.6 %all_to_all.30 = bf16[4,60,384]{2,1,0:T(8,128)(2,1)S(1)} all-to-all(bf16[4,60,384]{2,1,0:T(8,128)(2,1)S(1)} %reshape.185), channel_id=1, replica_groups=mesh['segment'=2,'expert'=4,'pair'=4] {'expert'}, dimensions={0} | all-to-all | bytes 368640 | tf_op jit(solution)/shard_map/all_to_all | solution.py:41
  26.4 12.1 %all_gather.9 = bf16[240,2,768]{0,1,2:T(2,128)(2,1)S(1)} all-gather(bf16[240,2,192]{0,1,2:T(2,128)(2,1)S(1)} %copy.19), channel_id=1, replica_groups=mesh['segment'=2,'expert'=4,'pair'=4] {'pair'}, dimensions={2}, use_global_device_ids=true | all-gather | bytes 921600 | tf_op jit(solution)/shard_map/all_gather | solution.py:48
  38.6 2.0 fusion.148
  40.5 2.3 copy.28
  43.0 1.6 copy.29
  49.0 40.5 %all-reduce.4.cloned.1.call-done = bf16[240,768]{1,0:T(8,128)(2,1)} async-done(((bf16[240,768]{1,0:T(8,128)(2,1)}), bf16[240,768]{1,0:T(8,128)(2,1)}) %all-reduce.4.cloned.1.call-update) | async-done | bytes 368656 | tf_op jit(solution)/shard_map/psum | solution.py:76
  89.5 1.2 fusion.37
  91.7 1.3 fusion.90
  93.6 4.6 %all-to-all-start.1 = ((bf16[4,60,192]{2,1,0:T(8,128)(2,1)}), bf16[4,60,192]{2,1,0:T(8,128)(2,1)S(1)}, u32[]{:S(2)}, u32[]{:S(2)}) async-start(bf16[4,60,192]{2,1,0:T(8,128)(2,1)} %reshape.187), calls=%async_computation.1 | async-start | bytes 262144 | tf_op jit(solution)/shard_map/all_to_all | solution.py:84
  98.2 6.0 %all-to-all-done.1 = bf16[4,60,192]{2,1,0:T(8,128)(2,1)S(1)} async-done(((bf16[4,60,192]{2,1,0:T(8,128)(2,1)}), bf16[4,60,192]{2,1,0:T(8,128)(2,1)S(1)}, u32[]{:S(2)}, u32[]{:S(2)}) %all-to-all-start.1) | async-done | bytes 92192 | tf_op jit(solution)/shard_map/all_to_all | solution.py:84
  105.4 1.3 collective-permute-start
  106.7 1.9 collective-permute-done
  109.7 1.9 convolution_convert_fusion.7
  111.5 1.6 reshape.189
  113.2 12.1 %all_to_all.31 = bf16[4,60,384]{2,1,0:T(8,128)(2,1)} all-to-all(bf16[4,60,384]{2,1,0:T(8,128)(2,1)} %reshape.189), channel_id=1, replica_groups=mesh['segment'=2,'expert'=4,'pair'=4] {'expert'}, dimensions={0} | all-to-all | bytes 368640 | tf_op jit(solution)/shard_map/all_to_all | solution.py:41
  126.4 1.3 copy.22
  127.7 11.8 %all_gather.10 = bf16[240,2,768]{0,1,2:T(2,128)(2,1)S(1)} all-gather(bf16[240,2,192]{0,1,2:T(2,128)(2,1)} %copy.22), channel_id=1, replica_groups=mesh['segment'=2,'expert'=4,'pair'=4] {'pair'}, dimensions={2}, use_global_device_ids=true | all-gather | bytes 921600 | tf_op jit(solution)/shard_map/all_gather | solution.py:48
  139.5 2.2 fusion.147
  141.8 2.2 copy.30
  144.1 1.4 fusion.49
  145.5 2.8 copy.31
  148.3 1.9 fusion.3
  151.9 3.2 %fusion.54 = f32[768,768]{1,0:T(8,128)} fusion(f32[240,768]{1,0:T(8,128)} %copy-done.3, bf16[240,1,768]{2,0,1:T(8,128)(2,1)S(1)} %copy-done.4), kind=kOutput, calls=%fused_computation.92 | convolution fusion | flops 284774400 | bytes 3465216 | tf_op jit(solution)/shard_map/dot_general | solution.py:63
  156.0 37.3 %all-reduce.6.cloned.1.call-done = bf16[240,768]{1,0:T(8,128)(2,1)} async-done(((bf16[240,768]{1,0:T(8,128)(2,1)}), bf16[240,768]{1,0:T(8,128)(2,1)}) %all-reduce.6.cloned.1.call-update) | async-done | bytes 368656 | tf_op jit(solution)/shard_map/psum | solution.py:76
  193.4 1.2 fusion.34
  195.6 1.3 fusion.88
  197.5 4.6 %all-to-all-start.3 = ((bf16[4,60,192]{2,1,0:T(8,128)(2,1)}), bf16[4,60,192]{2,1,0:T(8,128)(2,1)S(1)}, u32[]{:S(2)}, u32[]{:S(2)}) async-start(bf16[4,60,192]{2,1,0:T(8,128)(2,1)} %reshape.191), calls=%async_computation.3 | async-start | bytes 262144 | tf_op jit(solution)/shard_map/all_to_all | solution.py:84
  202.1 3.1 fusion.56
  205.2 2.9 all-to-all-done.3
  208.8 1.2 fusion.115
  210.1 1.6 collective-permute-start.1
  211.7 3.3 %fusion.55 = f32[768,768]{1,0:T(8,128)} fusion(f32[240,768]{1,0:T(8,128)} %fusion.49, bf16[240,1,768]{2,0,1:T(8,128)(2,1)S(1)} %copy-done.5), kind=kOutput, calls=%fused_computation.93 | convolution fusion | flops 284774400 | bytes 3465216 | tf_op jit(solution)/shard_map/dot_general | solution.py:63
  216.7 3.4 %all-to-all-start.4 = ((bf16[4,60,384]{2,1,0:T(8,128)(2,1)}), bf16[4,60,384]{2,1,0:T(8,128)(2,1)S(1)}, u32[]{:S(2)}, u32[]{:S(2)}) async-start(bf16[4,60,384]{2,1,0:T(8,128)(2,1)} %reshape.193), calls=%async_computation.4 | async-start | bytes 393216 | tf_op jit(solution)/shard_map/all_to_all | solution.py:41
  220.1 2.0 fusion.58
  222.8 5.0 %all-to-all-done.4 = bf16[4,60,384]{2,1,0:T(8,128)(2,1)S(1)} async-done(((bf16[4,60,384]{2,1,0:T(8,128)(2,1)}), bf16[4,60,384]{2,1,0:T(8,128)(2,1)S(1)}, u32[]{:S(2)}, u32[]{:S(2)}) %all-to-all-start.4) | async-done | bytes 184352 | tf_op jit(solution)/shard_map/all_to_all | solution.py:41
  228.8 13.4 %all_gather.11 = bf16[240,2,768]{0,1,2:T(2,128)(2,1)S(1)} all-gather(bf16[240,2,192]{0,1,2:T(2,128)(2,1)S(1)} %copy.25), channel_id=1, replica_groups=mesh['segment'=2,'expert'=4,'pair'=4] {'pair'}, dimensions={2}, use_global_device_ids=true | all-gather | bytes 921600 | tf_op jit(solution)/shard_map/all_gather | solution.py:48
  242.2 2.0 fusion.146
  244.2 2.2 copy.32
  246.5 1.4 fusion.52
  247.9 1.6 copy.33
  249.5 1.9 fusion.4
  253.5 4.1 %fusion.1 = bf16[1,1,768,768]{3,2,1,0:T(8,128)(2,1)} fusion(f32[768,768]{1,0:T(8,128)} %fusion.55, f32[768,768]{1,0:T(8,128)} %fusion.54, f32[]{:T(128)S(6)} %convert_element_type.239, f32[]{:T(128)S(6)} %convert_element_type.237, f32[]{:T(128)S(6)} %convert_element_type.235, f32[240,768]{1,0:T(8,128)S(1)} %copy-done.2, bf16[240,1,768]{2,0,1:T(8,128)(2,1)S(1)} %copy-done.6), kind=kOutput, calls=%fused_computation.3 | convolution fusion | flops 288313344 | bytes 7004172 | tf_op jit(solution)/shard_map/dot_general | solution.py:63
  257.7 37.0 %all-reduce.8.cloned.1.call-done = bf16[240,768]{1,0:T(8,128)(2,1)} async-done(((bf16[240,768]{1,0:T(8,128)(2,1)}), bf16[240,768]{1,0:T(8,128)(2,1)}) %all-reduce.8.cloned.1.call-update) | async-done | bytes 368656 | tf_op jit(solution)/shard_map/psum | solution.py:76
  294.6 1.2 fusion.31
  297.8 4.6 %all-to-all-start.5 = ((bf16[4,60,192]{2,1,0:T(8,128)(2,1)}), bf16[4,60,192]{2,1,0:T(8,128)(2,1)S(1)}, u32[]{:S(2)}, u32[]{:S(2)}) async-start(bf16[4,60,192]{2,1,0:T(8,128)(2,1)} %reshape.195), calls=%async_computation.5 | async-start | bytes 262144 | tf_op jit(solution)/shard_map/all_to_all | solution.py:84
  302.5 4.3 %fusion = bf16[1,1,768,768]{3,2,1,0:T(8,128)(2,1)} fusion(bf16[240,768]{1,0:T(8,128)(2,1)} %copy-done.16, f32[768,768]{1,0:T(8,128)} %fusion.58, f32[768,768]{1,0:T(8,128)} %fusion.56, f32[]{:T(128)S(6)} %convert_element_type.239, f32[]{:T(128)S(6)} %convert_element_type.237, f32[]{:T(128)S(6)} %convert_element_type.235, bf16[240,1,768]{2,0,1:T(8,128)(2,1)S(1)} %copy.32, ...), kind=kOutput, calls=%fused_computation.2 | convolution fusion | flops 287207424 | bytes 6636492 | tf_op jit(solution)/shard_map/dot_general | solution.py:60
  306.7 1.7 all-to-all-done.5
  (104 shorter events, 27.2 us)
Async XLA Ops:
  7.2 37.9 %copy-start = (bf16[1,1,768,768]{3,2,1,0:T(8,128)(2,1)S(1)}, bf16[1,1,768,768]{3,2,1,0:T(8,128)(2,1)}, u32[]{:S(2)}) copy-start(bf16[1,1,768,768]{3,2,1,0:T(8,128)(2,1)} %param.13) | copy-start | bytes 3538948
  7.2 82.3 %all-reduce.4.cloned.1.call-start = ((), (), s32[]{:S(2)}) async-start(), calls=%async_computation.6 | async-start | bytes 737280 | tf_op jit(solution)/shard_map/psum | solution.py:76
  40.5 4.0 %copy-start.1 = (bf16[1,1,768,768]{3,2,1,0:T(8,128)(2,1)S(1)}, bf16[1,1,768,768]{3,2,1,0:T(8,128)(2,1)}, u32[]{:S(2)}) copy-start(bf16[1,1,768,768]{3,2,1,0:T(8,128)(2,1)} %param.12) | copy-start | bytes 3538948
  44.6 1.0 copy-start.4
  45.6 0.9 copy-start.3
  46.4 0.8 copy-start.13
  93.6 10.6 %all-to-all-start.1 = ((bf16[4,60,192]{2,1,0:T(8,128)(2,1)}), bf16[4,60,192]{2,1,0:T(8,128)(2,1)S(1)}, u32[]{:S(2)}, u32[]{:S(2)}) async-start(bf16[4,60,192]{2,1,0:T(8,128)(2,1)} %reshape.187), calls=%async_computation.1 | async-start | bytes 262144 | tf_op jit(solution)/shard_map/all_to_all | solution.py:84
  98.2 95.1 %all-reduce.6.cloned.1.call-start = ((), (), s32[]{:S(2)}) async-start(), calls=%async_computation.7 | async-start | bytes 737280 | tf_op jit(solution)/shard_map/psum | solution.py:76
  105.4 7.7 %copy-start.7 = (bf16[2,192,192]{2,1,0:T(8,128)(2,1)}, bf16[2,192,192]{2,1,0:T(8,128)(2,1)S(1)}, u32[]{:S(2)}) copy-start(bf16[2,192,192]{2,1,0:T(8,128)(2,1)S(1)} %get-tuple-element.30) | copy-start | bytes 442372
  105.4 3.2 %collective-permute-start = (bf16[192,192]{1,0:T(8,128)(2,1)S(1)}, bf16[192,192]{1,0:T(8,128)(2,1)S(1)}, u32[]{:S(2)}, u32[]{:S(2)}) collective-permute-start(bf16[192,192]{1,0:T(8,128)(2,1)S(1)} %get-tuple-element.31), channel_id=1, source_target_pairs={{16,0},{17,1},{18,2},{19,3},{20,4},{21,5},{22,6},{23,7},{24,8},{25... | collective-permute-start | bytes 221192 | tf_op jit(solution)/shard_map/ppermute | solution.py:10
  108.6 4.5 %copy-start.22 = (bf16[192,192]{1,0:T(8,128)(2,1)}, bf16[192,192]{1,0:T(8,128)(2,1)S(1)}, u32[]{:S(2)}) copy-start(bf16[192,192]{1,0:T(8,128)(2,1)S(1)} %collective-permute-done) | copy-start | bytes 221188
  150.2 0.8 copy-start.14
  197.5 10.6 %all-to-all-start.3 = ((bf16[4,60,192]{2,1,0:T(8,128)(2,1)}), bf16[4,60,192]{2,1,0:T(8,128)(2,1)S(1)}, u32[]{:S(2)}, u32[]{:S(2)}) async-start(bf16[4,60,192]{2,1,0:T(8,128)(2,1)} %reshape.191), calls=%async_computation.3 | async-start | bytes 262144 | tf_op jit(solution)/shard_map/all_to_all | solution.py:84
  202.1 6.7 %copy-start.8 = (bf16[2,192,192]{2,1,0:T(8,128)(2,1)S(1)}, bf16[2,192,192]{2,1,0:T(8,128)(2,1)}, u32[]{:S(2)}) copy-start(bf16[2,192,192]{2,1,0:T(8,128)(2,1)} %copy-done.7) | copy-start | bytes 442372
  205.2 6.5 %copy-start.5 = (bf16[240,1,768]{2,0,1:T(8,128)(2,1)S(1)}, bf16[240,1,768]{2,0,1:T(8,128)(2,1)}, u32[]{:S(2)}) copy-start(bf16[240,1,768]{2,0,1:T(8,128)(2,1)} %copy.31) | copy-start | bytes 1105924
  210.1 12.1 %copy-start.9 = (bf16[2,192,192]{2,1,0:T(8,128)(2,1)}, bf16[2,192,192]{2,1,0:T(8,128)(2,1)S(1)}, u32[]{:S(2)}) copy-start(bf16[2,192,192]{2,1,0:T(8,128)(2,1)S(1)} %get-tuple-element.32) | copy-start | bytes 442372
  210.1 4.9 %copy-start.11 = (bf16[2,192,192]{2,1,0:T(8,128)(2,1)S(1)}, bf16[2,192,192]{2,1,0:T(8,128)(2,1)}, u32[]{:S(2)}) copy-start(bf16[2,192,192]{2,1,0:T(8,128)(2,1)} %param.8) | copy-start | bytes 442372
  210.1 5.6 %copy-start.19 = (bf16[192,192]{1,0:T(8,128)(2,1)S(1)}, bf16[192,192]{1,0:T(8,128)(2,1)}, u32[]{:S(2)}) copy-start(bf16[192,192]{1,0:T(8,128)(2,1)} %get-tuple-element.21) | copy-start | bytes 221188
  210.1 4.9 %collective-permute-start.1 = (bf16[192,192]{1,0:T(8,128)(2,1)S(1)}, bf16[192,192]{1,0:T(8,128)(2,1)S(1)}, u32[]{:S(2)}, u32[]{:S(2)}) collective-permute-start(bf16[192,192]{1,0:T(8,128)(2,1)S(1)} %get-tuple-element.33), channel_id=1, source_target_pairs={{16,0},{17,1},{18,2},{19,3},{20,4},{21,5},{22,6},{23,7},{24,8},{25... | collective-permute-start | bytes 221192 | tf_op jit(solution)/shard_map/ppermute | solution.py:10
  215.0 5.1 %copy-start.15 = (bf16[240,768]{1,0:T(8,128)(2,1)S(1)}, bf16[240,768]{1,0:T(8,128)(2,1)}, u32[]{:S(2)}) copy-start(bf16[240,768]{1,0:T(8,128)(2,1)} %copy-done.14) | copy-start | bytes 1105924
  215.0 0.6 copy-start.20
  216.7 11.2 %all-to-all-start.4 = ((bf16[4,60,384]{2,1,0:T(8,128)(2,1)}), bf16[4,60,384]{2,1,0:T(8,128)(2,1)S(1)}, u32[]{:S(2)}, u32[]{:S(2)}) async-start(bf16[4,60,384]{2,1,0:T(8,128)(2,1)} %reshape.193), calls=%async_computation.4 | async-start | bytes 393216 | tf_op jit(solution)/shard_map/all_to_all | solution.py:41
  220.0 74.6 %all-reduce.8.cloned.1.call-start = ((), (), s32[]{:S(2)}) async-start(), calls=%async_computation.8 | async-start | bytes 737280 | tf_op jit(solution)/shard_map/psum | solution.py:76
  251.4 0.8 copy-start.16
  252.2 1.2 copy-start.2
  252.2 1.3 copy-start.6
  297.8 10.6 %all-to-all-start.5 = ((bf16[4,60,192]{2,1,0:T(8,128)(2,1)}), bf16[4,60,192]{2,1,0:T(8,128)(2,1)S(1)}, u32[]{:S(2)}, u32[]{:S(2)}) async-start(bf16[4,60,192]{2,1,0:T(8,128)(2,1)} %reshape.195), calls=%async_computation.5 | async-start | bytes 262144 | tf_op jit(solution)/shard_map/all_to_all | solution.py:84
  302.4 6.0 %copy-start.10 = (bf16[2,192,192]{2,1,0:T(8,128)(2,1)S(1)}, bf16[2,192,192]{2,1,0:T(8,128)(2,1)}, u32[]{:S(2)}) copy-start(bf16[2,192,192]{2,1,0:T(8,128)(2,1)} %copy-done.9) | copy-start | bytes 442372
  302.4 6.0 %copy-start.12 = (bf16[2,192,192]{2,1,0:T(8,128)(2,1)S(1)}, bf16[2,192,192]{2,1,0:T(8,128)(2,1)}, u32[]{:S(2)}) copy-start(bf16[2,192,192]{2,1,0:T(8,128)(2,1)} %param.8) | copy-start | bytes 442372
  302.4 6.0 %copy-start.17 = (bf16[1,2,192,192]{3,2,1,0:T(8,128)(2,1)S(1)}, bf16[1,2,192,192]{3,2,1,0:T(8,128)(2,1)}, u32[]{:S(2)}) copy-start(bf16[1,2,192,192]{3,2,1,0:T(8,128)(2,1)} %copy.39) | copy-start | bytes 442372
  302.4 6.1 %copy-start.21 = (bf16[192,192]{1,0:T(8,128)(2,1)S(1)}, bf16[192,192]{1,0:T(8,128)(2,1)}, u32[]{:S(2)}) copy-start(bf16[192,192]{1,0:T(8,128)(2,1)} %copy-done.20) | copy-start | bytes 221188
  308.8 0.7 copy-start.18
Sparse Core Ops, SparseCore 0:
  48.2 41.2 all-reduce.3
  152.0 41.3 all-reduce.5
  253.2 41.3 all-reduce.7
where the time goes:
time: 318 us; the launch traced here: 316 us
  waiting for transfers between devices  132 us (42%)
  blocking collectives  63.1 us (20%)
  matrix products  35.2 us (11%)
  local copies, waits for them, and re-layouts  33.8 us (11%)
  starting transfers between devices  20.1 us (6%)
  other arithmetic  17.2 us (5%)
  between operations  14.2 us (4%)
    psum x3, waiting for transfers between devices, layer_pass(): lax.psum(partial_value.astype(jnp.bfloat16), 'pair').astype(jnp.float32)  115 us
    all_gather x3, blocking collectives, layer_pass(): lax.all_gather(arrived.reshape(slot_rows, 2, feat_share), 'pair', axis=2,...  37.4 us
    all_to_all x2, blocking collectives, layer_pass(): lax.all_to_all(packed.reshape(expert_count, capacity, 2 * feat_share), 'e...  25.7 us
    unnamed x53, local copies, waits for them, and re-layouts  15.7 us
    all_to_all x3, starting transfers between devices, layer_pass(): lax.all_to_all(branch.reshape(expert_count, capacity, feat_share), 'exper...  13.8 us
    dot_general x3, matrix products, layer_pass(): lax.dot_general(hidden, slot_grad, (((0,), (0,)), ((), ())), preferred_el...  10.7 us
    all_to_all x3, waiting for transfers between devices, layer_pass(): lax.all_to_all(branch.reshape(expert_count, capacity, feat_share), 'exper...  10.6 us
    dot_general x3, matrix products, layer_pass(): lax.dot_general(normed, back_pre, (((0,), (0,)), ((), ())), preferred_ele...  9.4 us
  transfers between devices with their start and end apart: 9, of which 8 were waited for; matrix products, arithmetic and copies ran while one was open for 7% of the time, Pallas kernels for 0%

commit v1 on v0

v1 whole, which is shorter than its diff:
```python
import functools

import jax
import jax.numpy as jnp
from jax import lax
from jax.experimental import pallas as pl
from jax.experimental.pallas import tpu as pltpu
from jax.sharding import PartitionSpec as P

BF = jnp.bfloat16
F32 = jnp.float32
MESH = pl.DeviceIdType.MESH


def repeat(count, step):
    if count <= 4:
        for i in range(count):
            step(i)
    else:
        lax.fori_loop(0, count, lambda i, c: (step(i), c)[1], 0)


def dot(a, b, ca, cb):
    return lax.dot_general(a, b, (((ca,), (cb,)), ((), ())), preferred_element_type=F32)


def eye(n):
    return lax.broadcasted_iota(jnp.int32, (n, n), 0) == lax.broadcasted_iota(jnp.int32, (n, n), 1)


def as_column(row):
    return jnp.sum(jnp.where(eye(row.shape[1]), row, 0.0), axis=1, keepdims=True)


def as_row(column):
    return jnp.sum(jnp.where(eye(column.shape[0]), column, 0.0), axis=0, keepdims=True)


def kernel(
    E, PN, cap, acts, cot, gates, owners, slots, win_h, wout_h, grads, gin_h, gout_h,
    win, wout, gin, gout, placing, zs_a, zs_g, gat_a, gat_g, xn, xg, inv_s, pre_s, slope_s, hid_s, bp_s,
    s_s, s_r, rs_s, rs_r, ret_s, ret_r, up_r,
    zsem_a, zrec_a, zsem_g, zrec_g, psem_a, prec_a, psem_g, prec_g,
    ssem, srec, rsem, rrec, tsem, trec, upsem, uprec, lsem,
):
    seg = lax.axis_index("segment")
    me = lax.axis_index("expert")
    mp = lax.axis_index("pair")
    M, T, F = cot.shape
    D = F * PN
    H = win.shape[1]
    R = E * cap
    B = M * cap
    groups = min(E, 4)
    ge = E // groups
    mg = me // ge

    load_in = pltpu.make_async_copy(win_h.at[0, 0], win, lsem.at[0])
    load_out = pltpu.make_async_copy(wout_h.at[0, 0], wout, lsem.at[1])
    load_in.start()
    load_out.start()

    barrier = pltpu.get_barrier_semaphore()

    def greet_e(k):
        pl.semaphore_signal(barrier, inc=1, device_id={"expert": lax.rem(me + k + 1, E)}, device_id_type=MESH)

    repeat(E - 1, greet_e)
    for k in range(1, PN):
        pl.semaphore_signal(barrier, inc=1, device_id={"pair": lax.rem(mp + k, PN)}, device_id_type=MESH)
    pl.semaphore_signal(barrier, inc=1, device_id={"segment": 1 - seg}, device_id_type=MESH)

    for m in range(M):
        target = owners[seg, pl.ds(m, 1), :] * cap + slots[seg, pl.ds(m, 1), :]
        placing[m] = (lax.broadcasted_iota(jnp.int32, (R, T), 0) == target).astype(BF)

    def pack(values, zs):
        rows = [dot(placing[m], values[m], 1, 0) for m in range(M)]
        zs[...] = jnp.concatenate(rows, axis=1).astype(BF).reshape(E, cap, M * F)

    def z_copy(zs, gat, ssems, rsems, d, src):
        return pltpu.make_async_remote_copy(
            src_ref=zs.at[d], dst_ref=gat.at[mp, src], send_sem=ssems.at[d], recv_sem=rsems.at[src],
            device_id={"expert": d}, device_id_type=MESH)

    def send_z(zs, gat, ssems, rsems):
        repeat(E - 1, lambda k: z_copy(zs, gat, ssems, rsems, lax.rem(me + k + 1, E), me).start())
        gat[mp, me] = zs[me]

    def p_copy(gat, ssems, rsems, q, src, g):
        part = gat.at[src, pl.ds(g * ge, ge)]
        return pltpu.make_async_remote_copy(
            src_ref=part, dst_ref=part, send_sem=ssems.at[q, g], recv_sem=rsems.at[src, g],
            device_id={"pair": q}, device_id_type=MESH)

    def forward(zs, gat, zsems, zrecs, psems, precs):
        def one(j):
            g = lax.rem(mg + j, groups)

            def arrive(i):
                e = g * ge + i

                @pl.when(e != me)
                def _():
                    z_copy(zs, gat, zsems, zrecs, e, e).wait_recv()

            repeat(ge, arrive)
            for k in range(1, PN):
                p_copy(gat, psems, precs, lax.rem(mp + k, PN), mp, g).start()

        repeat(groups, one)

    def gathered(gat, psems, precs, j):
        g = lax.rem(mg + j, groups)
        for k in range(1, PN):
            q = lax.rem(mp + k, PN)
            p_copy(gat, psems, precs, q, q, g).wait_recv()
        return g

    def finish(zs, gat, zsems, zrecs, psems, precs):
        repeat(E - 1, lambda k: z_copy(zs, gat, zsems, zrecs, lax.rem(me + k + 1, E), me).wait_send())

        def one(g):
            for k in range(1, PN):
                p_copy(gat, psems, precs, lax.rem(mp + k, PN), mp, g).wait_send()

        repeat(groups, one)

    a_set = (zs_a, gat_a, zsem_a, zrec_a, psem_a, prec_a)
    g_set = (zs_g, gat_g, zsem_g, zrec_g, psem_g, prec_g)

    pack([acts[seg, m] for m in range(M)], zs_a)
    pl.semaphore_wait(barrier, E - 1 + PN - 1 + 1)
    send_z(zs_a, gat_a, zsem_a, zrec_a)

    def send_grad():
        scaled = []
        for m in range(M):
            gate = as_column(gates[seg, pl.ds(m, 1), :])
            scaled.append((gate * up_r[m].astype(F32)).astype(BF))
        pack(scaled, zs_g)
        send_z(zs_g, gat_g, zsem_g, zrec_g)

    @pl.when(seg == 1)
    def _():
        up_r[...] = cot[...]
        send_grad()

    forward(*a_set)

    @pl.when(seg == 1)
    def _():
        forward(*g_set)

    def take_acts(j):
        g = gathered(gat_a, psem_a, prec_a, j)

        def block(i):
            e = g * ge + i
            parts = [gat_a[q, e].astype(F32) for q in range(PN)]
            for m in range(M):
                full = jnp.concatenate([v[:, m * F:(m + 1) * F] for v in parts], axis=1)
                scale = lax.rsqrt(jnp.mean(full * full, axis=1, keepdims=True) + 1e-06)
                rows = pl.ds(pl.multiple_of(e * B + m * cap, 16), cap)
                inv_s[rows, :] = scale
                xn[rows, :] = (full * scale).astype(BF)

        repeat(ge, block)

    repeat(groups, take_acts)
    load_in.wait()
    tile = 256 if H % 256 == 0 else 128
    chunk = min(M * R, 512)

    def tiles(step):
        def both(i):
            row = pl.ds(pl.multiple_of((i // (H // tile)) * chunk, 16), chunk)
            col = pl.ds(pl.multiple_of((i % (H // tile)) * tile, 128), tile)
            step(row, col)

        repeat((M * R // chunk) * (H // tile), both)

    def pre_step(row, col):
        u = dot(xn[row, :], win[:, col], 1, 0)
        square = u * u
        tangent = jnp.tanh(0.7978845608 * (u + 0.044715 * square * u))
        pre_s[row, col] = u
        hid_s[row, col] = (0.5 * u * (1.0 + tangent)).astype(BF)
        slope_s[row, col] = 0.5 * (1.0 + tangent) + 0.5 * u * (1.0 - tangent * tangent) * 0.7978845608 * (
            1.0 + 0.134145 * square)

    tiles(pre_step)
    load_out.wait()

    def up_copy():
        return pltpu.make_async_remote_copy(
            src_ref=grads.at[0], dst_ref=up_r, send_sem=upsem, recv_sem=uprec,
            device_id={"segment": 1 - seg}, device_id_type=MESH)

    @pl.when(seg == 0)
    def _():
        up_copy().wait_recv()
        send_grad()
        forward(*g_set)

    def take_grads(j):
        g = gathered(gat_g, psem_g, prec_g, j)

        def block(i):
            e = g * ge + i
            parts = [gat_g[q, e].astype(F32) for q in range(PN)]
            for m in range(M):
                full = jnp.concatenate([v[:, m * F:(m + 1) * F] for v in parts], axis=1)
                xg[pl.ds(pl.multiple_of(e * B + m * cap, 16), cap), :] = full.astype(BF)

        repeat(ge, block)

    repeat(groups, take_grads)

    def back_step(row, col):
        back = dot(xg[row, :], wout[col, :], 1, 1)
        bp_s[row, col] = (back * slope_s[row, col]).astype(BF)

    tiles(back_step)

    def r_copy(q, src, g):
        rows = pl.ds(g * ge, ge)
        return pltpu.make_async_remote_copy(
            src_ref=rs_s.at[q, rows], dst_ref=rs_r.at[src, rows], send_sem=rsem.at[q, g], recv_sem=rrec.at[src, g],
            device_id={"pair": q}, device_id_type=MESH)

    def s_copy(q, src):
        return pltpu.make_async_remote_copy(
            src_ref=s_s, dst_ref=s_r.at[src], send_sem=ssem.at[q], recv_sem=srec.at[src],
            device_id={"pair": q}, device_id_type=MESH)

    def partial_for(q, out):
        weights = win[pl.ds(pl.multiple_of(q * F, 16), F), :]

        def rows_step(i):
            part = dot(bp_s[pl.ds(pl.multiple_of(i * chunk, 16), chunk), :], weights, 1, 1)
            blocks = part.reshape(chunk // B, M, cap, F)
            joined = jnp.concatenate([blocks[:, m] for m in range(M)], axis=-1)
            out[q, pl.ds(i * (chunk // B), chunk // B)] = joined.astype(BF)

        repeat(M * R // chunk, rows_step)

    for k in range(1, PN):
        q = lax.rem(mp + k, PN)
        partial_for(q, rs_s)
        repeat(groups, lambda j: r_copy(q, mp, lax.rem(mg + 1 + j, groups)).start())

    def inner_step(e):
        rows = pl.ds(pl.multiple_of(e * B, 16), B)
        s_s[e] = as_row(jnp.sum(bp_s[rows, :].astype(F32) * pre_s[rows, :], axis=1, keepdims=True))

    repeat(E, inner_step)
    for k in range(1, PN):
        s_copy(lax.rem(mp + k, PN), mp).start()
    s_r[mp] = s_s[...]
    partial_for(mp, rs_r)

    def weight_grads():
        def one(i):
            col = pl.ds(pl.multiple_of(i * tile, 128), tile)
            gin[:, col] = dot(xn[...], bp_s[:, col], 0, 0).astype(BF)
            gout[col, :] = dot(hid_s[:, col], xg[...], 0, 0).astype(BF)

        repeat(H // tile, one)

    weight_grads()
    put_in = pltpu.make_async_copy(gin, gin_h.at[0, 0], lsem.at[2])
    put_out = pltpu.make_async_copy(gout, gout_h.at[0, 0], lsem.at[3])
    put_in.start()
    put_out.start()

    def t_copy(d, src):
        return pltpu.make_async_remote_copy(
            src_ref=ret_s.at[d], dst_ref=ret_r.at[src], send_sem=tsem.at[d], recv_sem=trec.at[src],
            device_id={"expert": d}, device_id_type=MESH)

    for k in range(1, PN):
        q = lax.rem(mp + k, PN)
        s_copy(q, q).wait_recv()

    def give_back(j):
        g = lax.rem(mg + 1 + j, groups)
        for k in range(1, PN):
            q = lax.rem(mp + k, PN)
            r_copy(q, q, g).wait_recv()

        def block(i):
            e = g * ge + i
            total = rs_r[0, e].astype(F32)
            inner = s_r[0, e]
            for q in range(1, PN):
                total = total + rs_r[q, e].astype(F32)
                inner = inner + s_r[q, e]
            inner = as_column(inner)
            own = gat_a[mp, e].astype(F32)
            pieces = []
            for m in range(M):
                scale = inv_s[pl.ds(pl.multiple_of(e * B + m * cap, 16), cap), :]
                lanes = slice(m * F, (m + 1) * F)
                factor = scale * scale * inner[m * cap:(m + 1) * cap] / D
                pieces.append(scale * total[:, lanes] - factor * own[:, lanes])
            ret_s[e] = jnp.concatenate(pieces, axis=1).astype(BF)

            @pl.when(e != me)
            def _():
                t_copy(e, me).start()

        repeat(ge, block)

    repeat(groups, give_back)
    ret_r[me] = ret_s[me]

    def back_arrive(k):
        src = lax.rem(me + k + 1, E)
        t_copy(src, src).wait_recv()

    repeat(E - 1, back_arrive)
    returned = ret_r[...].reshape(R, M * F)
    for m in range(M):
        restored = dot(placing[m], returned[:, m * F:(m + 1) * F], 0, 0)
        grads[0, m] = (up_r[m].astype(F32) + restored).astype(BF)

    @pl.when(seg == 1)
    def _():
        up_copy().start()

    finish(*a_set)
    finish(*g_set)
    for k in range(1, PN):
        q = lax.rem(mp + k, PN)
        s_copy(q, mp).wait_send()
        repeat(groups, lambda g: r_copy(q, mp, g).wait_send())
    repeat(E - 1, lambda k: t_copy(lax.rem(me + k + 1, E), me).wait_send())
    put_in.wait()
    put_out.wait()

    @pl.when(seg == 1)
    def _():
        up_copy().wait_send()


def body(acts, cotangent, gates, owners, slots, w_in, w_out):
    E = lax.axis_size("expert")
    PN = lax.axis_size("pair")
    M, T, F = cotangent.shape
    D, H = w_in.shape[2:]
    capacity = max(2, (5 * T + 4 * E - 1) // (4 * E))
    cap = (capacity + 15) // 16 * 16
    R = E * cap
    W = M * F
    groups = min(E, 4)
    vm = pltpu.VMEM
    dma = pltpu.SemaphoreType.DMA
    scratch = [
        vm((D, H), BF), vm((H, D), BF), vm((D, H), BF), vm((H, D), BF),
        vm((M, R, T), BF), vm((E, cap, W), BF), vm((E, cap, W), BF),
        vm((PN, E, cap, W), BF), vm((PN, E, cap, W), BF),
        vm((M * R, D), BF), vm((M * R, D), BF), vm((M * R, 1), F32),
        vm((M * R, H), F32), vm((M * R, H), F32), vm((M * R, H), BF), vm((M * R, H), BF),
        vm((E, 1, M * cap), F32), vm((PN, E, 1, M * cap), F32),
        vm((PN, E, cap, W), BF), vm((PN, E, cap, W), BF),
        vm((E, cap, W), BF), vm((E, cap, W), BF), vm((M, T, F), BF),
        dma((E,)), dma((E,)), dma((E,)), dma((E,)),
        dma((PN, groups)), dma((PN, groups)), dma((PN, groups)), dma((PN, groups)),
        dma((PN,)), dma((PN,)), dma((PN, groups)), dma((PN, groups)),
        dma((E,)), dma((E,)), dma(()), dma(()), dma((4,)),
    ]
    whole = pl.BlockSpec(memory_space=pltpu.VMEM)
    away = pl.BlockSpec(memory_space=pl.ANY)
    return pl.pallas_call(
        functools.partial(kernel, E, PN, cap),
        out_shape=(
            jax.ShapeDtypeStruct((1, M, T, F), BF),
            jax.ShapeDtypeStruct((1, 1, D, H), BF),
            jax.ShapeDtypeStruct((1, 1, H, D), BF),
        ),
        in_specs=[whole] * 5 + [away] * 2,
        out_specs=(whole, away, away),
        scratch_shapes=scratch,
        compiler_params=pltpu.CompilerParams(
            collective_id=0, has_side_effects=True, vmem_limit_bytes=56 * 1024 * 1024),
        cost_estimate=pl.CostEstimate(
            flops=10 * M * R * D * H, bytes_accessed=8 * D * H, transcendentals=M * R * H),
    )(acts, cotangent, gates, owners, slots, w_in, w_out)


def solution(mesh):
    placed = (
        P(None, None, "expert", "pair"),
        P(None, "expert", "pair"),
        P(None, None, "expert"),
        P(None, None, "expert"),
        P(None, None, "expert"),
        P("segment", "expert", None, "pair"),
        P("segment", "expert", "pair", None),
    )
    return jax.shard_map(
        body,
        mesh=mesh,
        in_specs=placed,
        out_specs=(
            P("segment", None, "expert", "pair"),
            P("segment", "expert", None, "pair"),
            P("segment", "expert", "pair", None),
        ),
        check_vma=False,
    )
```

time: 318 us -> 69.3 us (0.22)
  waiting for transfers between devices: 132 us -> 0 us
  Pallas kernels: 0 us -> 63.4 us
  blocking collectives: 63.1 us -> 0 us
  matrix products: 35.2 us -> 0 us
  local copies, waits for them, and re-layouts: 33.8 us -> 5.09 us
  starting transfers between devices: 20.1 us -> 0 us
  other arithmetic: 17.2 us -> 0 us
  between operations: 14.2 us -> 0.64 us
    psum x3 -> x0, waiting for transfers between devices: 115 us -> none  [layer_pass(): lax.psum(partial_value.astype(jnp.bfloat16), 'pair').astype(jnp.float32)]
    pallas_call x0 -> x1, Pallas kernels: none -> 63.4 us  [body(): pl.pallas_call(functools.partial(kernel, E, PN, cap), out_shape=(jax.Shap...]
    all_gather x3 -> x0, blocking collectives: 37.4 us -> none  [layer_pass(): lax.all_gather(arrived.reshape(slot_rows, 2, feat_share), 'pair', axis=2,...]
    dot_general x24 -> x0, matrix products: 35.2 us -> none  [the longest x3 10.7 us: layer_pass(): lax.dot_general(hidden, slot_grad, (((0,), (0,)), ((), ())), preferred_el...]
    all_to_all x2 -> x0, blocking collectives: 25.7 us -> none  [layer_pass(): lax.all_to_all(packed.reshape(expert_count, capacity, 2 * feat_share), 'e...]
    all_to_all x4 -> x0, starting transfers between devices: 17.2 us -> none  [the longest x3 13.8 us: layer_pass(): lax.all_to_all(branch.reshape(expert_count, capacity, feat_share), 'exper...]
    all_to_all x4 -> x0, waiting for transfers between devices: 15.6 us -> none  [the longest x3 10.6 us: layer_pass(): lax.all_to_all(branch.reshape(expert_count, capacity, feat_share), 'exper...]
    convert_element_type x15 -> x0, other arithmetic: 12.4 us -> none  [the longest x3 3.13 us: layer_pass(): lax.psum(partial_value.astype(jnp.bfloat16), 'pair').astype(jnp.float32)]
  transfers between devices with their start and end apart: 9 -> 0, of which waited for: 8 -> 0; matrix products, arithmetic and copies ran while one was open for 7% -> 0% of each run, Pallas kernels for 0% -> 0%
where the time goes in v1:
time: 69.3 us; the launch traced here: 69.1 us
  Pallas kernels  63.4 us (91%)
  local copies, waits for them, and re-layouts  5.09 us (7%)
    pallas_call x1, Pallas kernels, body(): pl.pallas_call(functools.partial(kernel, E, PN, cap), out_shape=(jax.Shap...  63.4 us
    unnamed x5, local copies, waits for them, and re-layouts  5.09 us

profile of v1, /device:TPU:0, one launch (start us, length us, event | category | flops | bytes accessed | tf_op | source)
XLA Modules:
  0.0 69.1 jit_solution(8375984947319621355)
XLA Ops:
  0.6 63.4 %shard_map.94 = (bf16[1,2,192,192]{3,2,1,0:T(8,128)(2,1)}, bf16[1,1,768,768]{3,2,1,0:T(8,128)(2,1)}, bf16[1,1,768,768]{3,2,1,0:T(8,128)(2,1)}) custom-call(bf16[2,2,192,192]{3,2,1,0:T(8,128)(2,1)} %acts.1, bf16[2,192,192]{2,1,0:T(8,128)(2,1)} %cot.1, f32[2,2,192]{2,1,0:T(2,128)} %gates.1, s32[2,2,192]{2,1,0:T(2,128)} %owners.1, s32[2,2,192]{2,1,0:T(2,128)} %slots.1, ...), custom_call_target="tpu_custom_call" | custom-call | flops 3019898880 | bytes 4718592 | tf_op jit(solution)/shard_map/pallas_call | solution.py:375
  64.0 1.6 %copy.13 = bf16[1,2,192,192]{3,2,1,0:T(8,128)(2,1)} copy(bf16[1,2,192,192]{3,2,1,0:T(8,128)(2,1)} %get-tuple-element.6) | data formatting | bytes 294912
  65.6 0.0 copy-start
  65.6 2.5 %copy.14 = bf16[1,1,768,768]{3,2,1,0:T(8,128)(2,1)} copy(bf16[1,1,768,768]{3,2,1,0:T(8,128)(2,1)} %get-tuple-element.7) | data formatting | bytes 2359296
  68.1 0.0 copy-done
  68.1 1.0 %copy.15 = bf16[1,1,768,768]{3,2,1,0:T(8,128)(2,1)} copy(bf16[1,1,768,768]{3,2,1,0:T(8,128)(2,1)S(1)} %copy-done) | data formatting | bytes 2359296
Async XLA Ops:
  65.6 2.5 %copy-start = (bf16[1,1,768,768]{3,2,1,0:T(8,128)(2,1)S(1)}, bf16[1,1,768,768]{3,2,1,0:T(8,128)(2,1)}, u32[]{:S(2)}) copy-start(bf16[1,1,768,768]{3,2,1,0:T(8,128)(2,1)} %get-tuple-element.8) | copy-start | bytes 3538948

commit v2 on v1

v2 whole, which is shorter than its diff:
```python
import functools

import jax
import jax.numpy as jnp
from jax import lax
from jax.experimental import pallas as pl
from jax.experimental.pallas import tpu as pltpu
from jax.sharding import PartitionSpec as P

BF = jnp.bfloat16
F32 = jnp.float32
MESH = pl.DeviceIdType.MESH


def repeat(count, step):
    if count <= 4:
        for i in range(count):
            step(i)
    else:
        lax.fori_loop(0, count, lambda i, c: (step(i), c)[1], 0)


def dot(a, b, ca, cb):
    return lax.dot_general(a, b, (((ca,), (cb,)), ((), ())), preferred_element_type=F32)


def eye(n):
    return lax.broadcasted_iota(jnp.int32, (n, n), 0) == lax.broadcasted_iota(jnp.int32, (n, n), 1)


def as_column(row):
    return jnp.sum(jnp.where(eye(row.shape[1]), row, 0.0), axis=1, keepdims=True)


def as_row(column):
    return jnp.sum(jnp.where(eye(column.shape[0]), column, 0.0), axis=0, keepdims=True)


def kernel(
    E, PN, cap, acts, cot, gates, owners, slots, win_h, wout_h, grads, gin_h, gout_h,
    win, wout, gin, gout, placing, zs_a, zs_g, gat_a, gat_g, xn, xg, inv_s, pre_s, slope_s, hid_s, bp_s,
    s_s, s_r, rs_s, rs_r, ret_s, ret_r, up_r, gate_s, inner_s,
    zsem_a, zrec_a, zsem_g, zrec_g, psem_a, prec_a, psem_g, prec_g,
    ssem, srec, rsem, rrec, tsem, trec, upsem, uprec, lsem, go_sem,
):
    seg = lax.axis_index("segment")
    me = lax.axis_index("expert")
    mp = lax.axis_index("pair")
    M, T, F = cot.shape
    D = F * PN
    H = win.shape[1]
    R = E * cap
    B = M * cap
    groups = min(E, 4)
    ge = E // groups
    mg = me // ge

    load_in = pltpu.make_async_copy(win_h.at[0, 0], win, lsem.at[0])
    load_out = pltpu.make_async_copy(wout_h.at[0, 0], wout, lsem.at[1])
    load_in.start()
    load_out.start()

    barrier = pltpu.get_barrier_semaphore()

    def greet_e(k):
        pl.semaphore_signal(barrier, inc=1, device_id={"expert": lax.rem(me + k + 1, E)}, device_id_type=MESH)

    repeat(E - 1, greet_e)
    for k in range(1, PN):
        pl.semaphore_signal(barrier, inc=1, device_id={"pair": lax.rem(mp + k, PN)}, device_id_type=MESH)
    pl.semaphore_signal(barrier, inc=1, device_id={"segment": 1 - seg}, device_id_type=MESH)

    for m in range(M):
        target = owners[seg, pl.ds(m, 1), :] * cap + slots[seg, pl.ds(m, 1), :]
        placing[m] = (lax.broadcasted_iota(jnp.int32, (R, T), 0) == target).astype(BF)

    def pack(values, zs):
        rows = [dot(placing[m], values[m], 1, 0) for m in range(M)]
        zs[...] = jnp.concatenate(rows, axis=1).astype(BF).reshape(E, cap, M * F)

    def z_copy(zs, gat, ssems, rsems, d, src):
        return pltpu.make_async_remote_copy(
            src_ref=zs.at[d], dst_ref=gat.at[mp, src], send_sem=ssems.at[d], recv_sem=rsems.at[src],
            device_id={"expert": d}, device_id_type=MESH)

    def send_z(zs, gat, ssems, rsems):
        repeat(E - 1, lambda k: z_copy(zs, gat, ssems, rsems, lax.rem(me + k + 1, E), me).start())
        gat[mp, me] = zs[me]

    def p_copy(gat, ssems, rsems, q, src, g):
        part = gat.at[src, pl.ds(g * ge, ge)]
        return pltpu.make_async_remote_copy(
            src_ref=part, dst_ref=part, send_sem=ssems.at[q, g], recv_sem=rsems.at[src, g],
            device_id={"pair": q}, device_id_type=MESH)

    def forward(zs, gat, zsems, zrecs, psems, precs, j):
        g = lax.rem(mg + groups - j, groups)

        def arrive(i):
            e = g * ge + i

            @pl.when(e != me)
            def _():
                z_copy(zs, gat, zsems, zrecs, e, e).wait_recv()

        repeat(ge, arrive)
        for k in range(PN - 1, 0, -1):
            p_copy(gat, psems, precs, lax.rem(mp + k, PN), mp, g).start()

    def gathered(gat, psems, precs, j):
        g = lax.rem(mg + groups - j, groups)
        for k in range(1, PN):
            q = lax.rem(mp + k, PN)
            p_copy(gat, psems, precs, q, q, g).wait_recv()
        return g

    def finish(zs, gat, zsems, zrecs, psems, precs):
        repeat(E - 1, lambda k: z_copy(zs, gat, zsems, zrecs, lax.rem(me + k + 1, E), me).wait_send())

        def one(g):
            for k in range(1, PN):
                p_copy(gat, psems, precs, lax.rem(mp + k, PN), mp, g).wait_send()

        repeat(groups, one)

    a_set = (zs_a, gat_a, zsem_a, zrec_a, psem_a, prec_a)
    g_set = (zs_g, gat_g, zsem_g, zrec_g, psem_g, prec_g)
    unit = ge * B

    def go(i):
        pl.semaphore_signal(go_sem.at[i], inc=1, device_id={"segment": 1 - seg}, device_id_type=MESH)

    def send_grad():
        scaled = [(gate_s[m] * up_r[m].astype(F32)).astype(BF) for m in range(M)]
        pack(scaled, zs_g)
        send_z(zs_g, gat_g, zsem_g, zrec_g)

    def take(gat, psems, precs, j, use):
        g = gathered(gat, psems, precs, j)

        def block(i):
            e = g * ge + i
            parts = [gat[q, e].astype(F32) for q in range(PN)]
            for m in range(M):
                full = jnp.concatenate([v[:, m * F:(m + 1) * F] for v in parts], axis=1)
                use(pl.ds(pl.multiple_of(e * B + m * cap, 16), cap), full)

        repeat(ge, block)
        return g, pl.ds(pl.multiple_of(g * unit, 16), unit)

    def norm_rows(rows, full):
        scale = lax.rsqrt(jnp.mean(full * full, axis=1, keepdims=True) + 1e-06)
        inv_s[rows, :] = scale
        xn[rows, :] = (full * scale).astype(BF)

    def grad_rows(rows, full):
        xg[rows, :] = full.astype(BF)

    def r_copy(q, src, g):
        rows = pl.ds(g * ge, ge)
        return pltpu.make_async_remote_copy(
            src_ref=rs_s.at[q, rows], dst_ref=rs_r.at[src, rows], send_sem=rsem.at[q, g], recv_sem=rrec.at[src, g],
            device_id={"pair": q}, device_id_type=MESH)

    def s_copy(q, src, g):
        rows = pl.ds(g * ge, ge)
        return pltpu.make_async_remote_copy(
            src_ref=s_s.at[rows], dst_ref=s_r.at[src, rows], send_sem=ssem.at[q, g], recv_sem=srec.at[src, g],
            device_id={"pair": q}, device_id_type=MESH)

    def forward_pass(j):
        _, rows = take(gat_a, psem_a, prec_a, j, norm_rows)
        for t in range(H // tile):
            col = pl.ds(t * tile, tile)
            u = dot(xn[rows, :], win[:, col], 1, 0)
            square = u * u
            tangent = jnp.tanh(0.7978845608 * (u + 0.044715 * square * u))
            pre_s[rows, col] = u
            hid_s[rows, col] = (0.5 * u * (1.0 + tangent)).astype(BF)
            slope_s[rows, col] = 0.5 * (1.0 + tangent) + 0.5 * u * (1.0 - tangent * tangent) * 0.7978845608 * (
                1.0 + 0.134145 * square)

    def backward_pass(j):
        g, rows = take(gat_g, psem_g, prec_g, j, grad_rows)
        inner = jnp.zeros((unit, 1), F32)
        for t in range(H // tile):
            col = pl.ds(t * tile, tile)
            back = dot(xg[rows, :], wout[col, :], 1, 1)
            low = (back * slope_s[rows, col]).astype(BF)
            bp_s[rows, col] = low
            inner = inner + jnp.sum(low.astype(F32) * pre_s[rows, col], axis=1, keepdims=True)
        inner_s[rows, :] = inner

        def partial_for(q, out):
            weights = win[pl.ds(pl.multiple_of(q * F, 16), F), :]
            blocks = dot(bp_s[rows, :], weights, 1, 1).reshape(ge, M, cap, F)
            joined = jnp.concatenate([blocks[:, m] for m in range(M)], axis=-1)
            out[q, pl.ds(g * ge, ge)] = joined.astype(BF)

        for k in range(PN - 1, 0, -1):
            q = lax.rem(mp + k, PN)
            partial_for(q, rs_s)
            r_copy(q, mp, g).start()

        def inner_row(i):
            e = g * ge + i
            row = as_row(inner_s[pl.ds(pl.multiple_of(e * B, 16), B), :])
            s_s[e] = row
            s_r[mp, e] = row

        repeat(ge, inner_row)
        for k in range(1, PN):
            s_copy(lax.rem(mp + k, PN), mp, g).start()
        partial_for(mp, rs_r)

    def first_grad():
        for t in range(H // tile):
            col = pl.ds(t * tile, tile)
            gin[:, col] = dot(xn[...], bp_s[:, col], 0, 0).astype(BF)
        put_in.start()

    def second_grad():
        for t in range(H // tile):
            col = pl.ds(t * tile, tile)
            gout[col, :] = dot(hid_s[:, col], xg[...], 0, 0).astype(BF)
        put_out.start()

    def t_copy(d, src):
        return pltpu.make_async_remote_copy(
            src_ref=ret_s.at[d], dst_ref=ret_r.at[src], send_sem=tsem.at[d], recv_sem=trec.at[src],
            device_id={"expert": d}, device_id_type=MESH)

    def give_back(j):
        g = lax.rem(mg + groups - j, groups)
        for k in range(1, PN):
            q = lax.rem(mp + k, PN)
            r_copy(q, q, g).wait_recv()
            s_copy(q, q, g).wait_recv()

        def block(i):
            e = g * ge + i
            total = rs_r[0, e].astype(F32)
            inner = s_r[0, e]
            for q in range(1, PN):
                total = total + rs_r[q, e].astype(F32)
                inner = inner + s_r[q, e]
            inner = as_column(inner)
            own = gat_a[mp, e].astype(F32)
            pieces = []
            for m in range(M):
                scale = inv_s[pl.ds(pl.multiple_of(e * B + m * cap, 16), cap), :]
                lanes = slice(m * F, (m + 1) * F)
                factor = scale * scale * inner[m * cap:(m + 1) * cap] / D
                pieces.append(scale * total[:, lanes] - factor * own[:, lanes])
            ret_s[e] = jnp.concatenate(pieces, axis=1).astype(BF)

            @pl.when(e != me)
            def _():
                t_copy(e, me).start()

        repeat(ge, block)

    def up_copy():
        return pltpu.make_async_remote_copy(
            src_ref=grads.at[0], dst_ref=up_r, send_sem=upsem, recv_sem=uprec,
            device_id={"segment": 1 - seg}, device_id_type=MESH)

    def cycle(step):
        lax.fori_loop(0, groups, lambda j, c: (step(j), c)[1], 0)

    put_in = pltpu.make_async_copy(gin, gin_h.at[0, 0], lsem.at[2])
    put_out = pltpu.make_async_copy(gout, gout_h.at[0, 0], lsem.at[3])
    tile = 256 if H % 256 == 0 else 128
    pack([acts[seg, m] for m in range(M)], zs_a)
    for m in range(M):
        gate_s[m] = as_column(gates[seg, pl.ds(m, 1), :])
    pl.semaphore_wait(barrier, E - 1 + PN - 1 + 1)

    @pl.when(seg == 0)
    def _():
        pl.semaphore_wait(go_sem.at[0], 1)

    send_z(zs_a, gat_a, zsem_a, zrec_a)

    @pl.when(seg == 1)
    def _():
        up_r[...] = cot[...]
        send_grad()

    @pl.when(seg == 0)
    def _():
        pl.semaphore_wait(go_sem.at[1], 1)

    def both(j):
        forward(*a_set, j)

        @pl.when(seg == 1)
        def _():
            forward(*g_set, j)

    repeat(groups, both)

    @pl.when(seg == 1)
    def _():
        go(0)

    load_in.wait()
    load_out.wait()
    cycle(forward_pass)

    @pl.when(seg == 0)
    def _():
        up_copy().wait_recv()
        send_grad()
        repeat(groups, lambda j: forward(*g_set, j))

    cycle(backward_pass)

    @pl.when(seg == 0)
    def _():
        first_grad()

    cycle(give_back)
    ret_r[me] = ret_s[me]

    @pl.when(seg == 1)
    def _():
        go(1)

    @pl.when(seg == 0)
    def _():
        second_grad()

    def back_arrive(k):
        src = lax.rem(me + k + 1, E)
        t_copy(src, src).wait_recv()

    repeat(E - 1, back_arrive)
    returned = ret_r[...].reshape(R, M * F)
    for m in range(M):
        restored = dot(placing[m], returned[:, m * F:(m + 1) * F], 0, 0)
        grads[0, m] = (up_r[m].astype(F32) + restored).astype(BF)

    @pl.when(seg == 1)
    def _():
        up_copy().start()
        first_grad()
        second_grad()

    finish(*a_set)
    finish(*g_set)
    for k in range(1, PN):
        q = lax.rem(mp + k, PN)

        def sent(g):
            s_copy(q, mp, g).wait_send()
            r_copy(q, mp, g).wait_send()

        repeat(groups, sent)
    repeat(E - 1, lambda k: t_copy(lax.rem(me + k + 1, E), me).wait_send())
    put_in.wait()
    put_out.wait()

    @pl.when(seg == 1)
    def _():
        up_copy().wait_send()


def place_kernel(a, b, c, a_out, b_out, c_out, sem):
    copies = [pltpu.make_async_copy(a, a_out, sem.at[0])]
    step = b.shape[2] // 4
    for n, (src, dst) in enumerate(((b, b_out), (c, c_out))):
        for i in range(4):
            rows = pl.ds(i * step, step)
            copies.append(pltpu.make_async_copy(src.at[:, :, rows], dst.at[:, :, rows], sem.at[1 + 4 * n + i]))
    for copy in copies:
        copy.start()
    for copy in copies:
        copy.wait()


def body(acts, cotangent, gates, owners, slots, w_in, w_out):
    E = lax.axis_size("expert")
    PN = lax.axis_size("pair")
    M, T, F = cotangent.shape
    D, H = w_in.shape[2:]
    capacity = max(2, (5 * T + 4 * E - 1) // (4 * E))
    cap = (capacity + 15) // 16 * 16
    R = E * cap
    W = M * F
    groups = min(E, 4)
    vm = pltpu.VMEM
    dma = pltpu.SemaphoreType.DMA
    scratch = [
        vm((D, H), BF), vm((H, D), BF), vm((D, H), BF), vm((H, D), BF),
        vm((M, R, T), BF), vm((E, cap, W), BF), vm((E, cap, W), BF),
        vm((PN, E, cap, W), BF), vm((PN, E, cap, W), BF),
        vm((M * R, D), BF), vm((M * R, D), BF), vm((M * R, 1), F32),
        vm((M * R, H), F32), vm((M * R, H), F32), vm((M * R, H), BF), vm((M * R, H), BF),
        vm((E, 1, M * cap), F32), vm((PN, E, 1, M * cap), F32),
        vm((PN, E, cap, W), BF), vm((PN, E, cap, W), BF),
        vm((E, cap, W), BF), vm((E, cap, W), BF), vm((M, T, F), BF),
        vm((M, T, 1), F32), vm((M * R, 1), F32),
        dma((E,)), dma((E,)), dma((E,)), dma((E,)),
        dma((PN, groups)), dma((PN, groups)), dma((PN, groups)), dma((PN, groups)),
        dma((PN, groups)), dma((PN, groups)), dma((PN, groups)), dma((PN, groups)),
        dma((E,)), dma((E,)), dma(()), dma(()), dma((4,)), pltpu.SemaphoreType.REGULAR((2,)),
    ]
    whole = pl.BlockSpec(memory_space=pltpu.VMEM)
    away = pl.BlockSpec(memory_space=pl.ANY)
    shapes = (
            jax.ShapeDtypeStruct((1, M, T, F), BF),
            jax.ShapeDtypeStruct((1, 1, D, H), BF),
            jax.ShapeDtypeStruct((1, 1, H, D), BF),
    )
    held = pl.pallas_call(
        functools.partial(kernel, E, PN, cap),
        out_shape=shapes,
        in_specs=[whole] * 5 + [away] * 2,
        out_specs=(whole, away, away),
        scratch_shapes=scratch,
        compiler_params=pltpu.CompilerParams(
            collective_id=0, has_side_effects=True, vmem_limit_bytes=56 * 1024 * 1024),
        cost_estimate=pl.CostEstimate(
            flops=10 * M * R * D * H, bytes_accessed=8 * D * H, transcendentals=M * R * H),
    )(acts, cotangent, gates, owners, slots, w_in, w_out)
    return pl.pallas_call(
        place_kernel,
        out_shape=shapes,
        in_specs=[pl.BlockSpec(memory_space=pltpu.HBM)] * 3,
        out_specs=(pl.BlockSpec(memory_space=pltpu.HBM),) * 3,
        scratch_shapes=[dma((9,))],
        cost_estimate=pl.CostEstimate(flops=0, bytes_accessed=8 * D * H, transcendentals=0),
    )(*held)


def solution(mesh):
    placed = (
        P(None, None, "expert", "pair"),
        P(None, "expert", "pair"),
        P(None, None, "expert"),
        P(None, None, "expert"),
        P(None, None, "expert"),
        P("segment", "expert", None, "pair"),
        P("segment", "expert", "pair", None),
    )
    return jax.shard_map(
        body,
        mesh=mesh,
        in_specs=placed,
        out_specs=(
            P("segment", None, "expert", "pair"),
            P("segment", "expert", None, "pair"),
            P("segment", "expert", "pair", None),
        ),
        check_vma=False,
    )
```

time: 69.3 us -> 138 us (1.99)
  Pallas kernels: 63.4 us -> 138 us
  local copies, waits for them, and re-layouts: 5.09 us -> 0 us
    pallas_call x1 -> x2, Pallas kernels: 63.4 us -> 138 us  [the longest x1 78.6 us: body(): pl.pallas_call(place_kernel, out_shape=shapes, in_specs=[pl.BlockSpec(mem...]
    unnamed x5 -> x0, local copies, waits for them, and re-layouts: 5.09 us -> none
where the time goes in v2:
time: 138 us
  Pallas kernels  138 us (100%)
    pallas_call x1, Pallas kernels, body(): pl.pallas_call(place_kernel, out_shape=shapes, in_specs=[pl.BlockSpec(mem...  78.6 us
    pallas_call x1, Pallas kernels, body(): pl.pallas_call(functools.partial(kernel, E, PN, cap), out_shape=shapes, i...  59.1 us

profile of v2, /device:TPU:0, one launch (start us, length us, event | category | flops | bytes accessed | tf_op | source)
XLA Modules:
  0.0 138.4 jit_solution(14187426258800637637)
XLA Ops:
  0.6 59.1 %shard_map.94 = (bf16[1,2,192,192]{3,2,1,0:T(8,128)(2,1)}, bf16[1,1,768,768]{3,2,1,0:T(8,128)(2,1)}, bf16[1,1,768,768]{3,2,1,0:T(8,128)(2,1)}) custom-call(bf16[2,2,192,192]{3,2,1,0:T(8,128)(2,1)} %acts.1, bf16[2,192,192]{2,1,0:T(8,128)(2,1)} %cot.1, f32[2,2,192]{2,1,0:T(2,128)} %gates.1, s32[2,2,192]{2,1,0:T(2,128)} %owners.1, s32[2,2,192]{2,1,0:T(2,128)} %slots.1, ...), custom_call_target="tpu_custom_call" | custom-call | flops 3019898880 | bytes 4718592 | tf_op jit(solution)/shard_map/pallas_call | solution.py:416
  59.7 78.6 %shard_map.95 = (bf16[1,2,192,192]{3,2,1,0:T(8,128)(2,1)}, bf16[1,1,768,768]{3,2,1,0:T(8,128)(2,1)}, bf16[1,1,768,768]{3,2,1,0:T(8,128)(2,1)}) custom-call(bf16[1,2,192,192]{3,2,1,0:T(8,128)(2,1)} %get-tuple-element.6.a, bf16[1,1,768,768]{3,2,1,0:T(8,128)(2,1)} %get-tuple-element.7.b, bf16[1,1,768,768]{3,2,1,0:T(8,128)(2,1)} %get-tuple-element.8.c), custom_call_target="tpu_custom_call" | custom-call | bytes 4718592 | tf_op jit(solution)/shard_map/pallas_call | solution.py:427

commit v3 on v2

--- a/solution.py
+++ b/solution.py
@@ -39,7 +39,7 @@
 def kernel(
     E, PN, cap, acts, cot, gates, owners, slots, win_h, wout_h, grads, gin_h, gout_h,
     win, wout, gin, gout, placing, zs_a, zs_g, gat_a, gat_g, xn, xg, inv_s, pre_s, slope_s, hid_s, bp_s,
-    s_s, s_r, rs_s, rs_r, ret_s, ret_r, up_r, gate_s, inner_s,
+    s_s, s_r, rs_s, rs_r, ret_s, ret_r, up_r, gate_s, inner_s, xn_t, hid_t, placing_t,
     zsem_a, zrec_a, zsem_g, zrec_g, psem_a, prec_a, psem_g, prec_g,
     ssem, srec, rsem, rrec, tsem, trec, upsem, uprec, lsem, go_sem,
 ):
@@ -213,16 +213,22 @@
             s_copy(lax.rem(mp + k, PN), mp, g).start()
         partial_for(mp, rs_r)
 
+    def turn():
+        for t in range(D // 128):
+            xn_t[pl.ds(t * 128, 128), :] = jnp.transpose(xn[:, pl.ds(t * 128, 128)])
+        for t in range(H // 128):
+            hid_t[pl.ds(t * 128, 128), :] = jnp.transpose(hid_s[:, pl.ds(t * 128, 128)])
+
     def first_grad():
         for t in range(H // tile):
             col = pl.ds(t * tile, tile)
-            gin[:, col] = dot(xn[...], bp_s[:, col], 0, 0).astype(BF)
+            gin[:, col] = dot(xn_t[...], bp_s[:, col], 1, 0).astype(BF)
         put_in.start()
 
     def second_grad():
         for t in range(H // tile):
             col = pl.ds(t * tile, tile)
-            gout[col, :] = dot(hid_s[:, col], xg[...], 0, 0).astype(BF)
+            gout[col, :] = dot(hid_t[col, :], xg[...], 1, 0).astype(BF)
         put_out.start()
 
     def t_copy(d, src):
@@ -274,6 +280,9 @@
     pack([acts[seg, m] for m in range(M)], zs_a)
     for m in range(M):
         gate_s[m] = as_column(gates[seg, pl.ds(m, 1), :])
+        spot = owners[seg, pl.ds(m, 1), :] * cap + slots[seg, pl.ds(m, 1), :]
+        spot = as_column(spot.astype(F32)).astype(jnp.int32)
+        placing_t[m] = (lax.broadcasted_iota(jnp.int32, (T, R), 1) == spot).astype(BF)
     pl.semaphore_wait(barrier, E - 1 + PN - 1 + 1)
 
     @pl.when(seg == 0)
@@ -310,22 +319,23 @@
 
     @pl.when(seg == 0)
     def _():
+        turn()
         up_copy().wait_recv()
         send_grad()
         repeat(groups, lambda j: forward(*g_set, j))
 
     cycle(backward_pass)
 
+    @pl.when(seg == 1)
+    def _():
+        go(1)
+
     @pl.when(seg == 0)
     def _():
         first_grad()
 
     cycle(give_back)
     ret_r[me] = ret_s[me]
-
-    @pl.when(seg == 1)
-    def _():
-        go(1)
 
     @pl.when(seg == 0)
     def _():
@@ -338,12 +348,13 @@
     repeat(E - 1, back_arrive)
     returned = ret_r[...].reshape(R, M * F)
     for m in range(M):
-        restored = dot(placing[m], returned[:, m * F:(m + 1) * F], 0, 0)
+        restored = dot(placing_t[m], returned[:, m * F:(m + 1) * F], 1, 0)
         grads[0, m] = (up_r[m].astype(F32) + restored).astype(BF)
 
     @pl.when(seg == 1)
     def _():
         up_copy().start()
+        turn()
         first_grad()
         second_grad()
 
@@ -366,17 +377,10 @@
         up_copy().wait_send()
 
 
-def place_kernel(a, b, c, a_out, b_out, c_out, sem):
-    copies = [pltpu.make_async_copy(a, a_out, sem.at[0])]
-    step = b.shape[2] // 4
-    for n, (src, dst) in enumerate(((b, b_out), (c, c_out))):
-        for i in range(4):
-            rows = pl.ds(i * step, step)
-            copies.append(pltpu.make_async_copy(src.at[:, :, rows], dst.at[:, :, rows], sem.at[1 + 4 * n + i]))
-    for copy in copies:
-        copy.start()
-    for copy in copies:
-        copy.wait()
+def place_kernel(a, b, c, a_out, b_out, c_out):
+    a_out[...] = a[...]
+    b_out[...] = b[...]
+    c_out[...] = c[...]
 
 
 def body(acts, cotangent, gates, owners, slots, w_in, w_out):
@@ -401,6 +405,7 @@
         vm((PN, E, cap, W), BF), vm((PN, E, cap, W), BF),
         vm((E, cap, W), BF), vm((E, cap, W), BF), vm((M, T, F), BF),
         vm((M, T, 1), F32), vm((M * R, 1), F32),
+        vm((D, M * R), BF), vm((H, M * R), BF), vm((M, T, R), BF),
         dma((E,)), dma((E,)), dma((E,)), dma((E,)),
         dma((PN, groups)), dma((PN, groups)), dma((PN, groups)), dma((PN, groups)),
         dma((PN, groups)), dma((PN, groups)), dma((PN, groups)), dma((PN, groups)),
@@ -424,12 +429,18 @@
         cost_estimate=pl.CostEstimate(
             flops=10 * M * R * D * H, bytes_accessed=8 * D * H, transcendentals=M * R * H),
     )(acts, cotangent, gates, owners, slots, w_in, w_out)
+    steps = 4
+    slices = [
+        pl.BlockSpec((1, M, T // steps, F), lambda i: (0, 0, i, 0)),
+        pl.BlockSpec((1, 1, D // steps, H), lambda i: (0, 0, i, 0)),
+        pl.BlockSpec((1, 1, H // steps, D), lambda i: (0, 0, i, 0)),
+    ]
     return pl.pallas_call(
         place_kernel,
+        grid=(steps,),
         out_shape=shapes,
-        in_specs=[pl.BlockSpec(memory_space=pltpu.HBM)] * 3,
-        out_specs=(pl.BlockSpec(memory_space=pltpu.HBM),) * 3,
-        scratch_shapes=[dma((9,))],
+        in_specs=slices,
+        out_specs=tuple(slices),
         cost_estimate=pl.CostEstimate(flops=0, bytes_accessed=8 * D * H, transcendentals=0),
     )(*held)
 

time: 138 us -> 61.9 us (0.45)
  Pallas kernels: 138 us -> 61 us
    pallas_call x1, Pallas kernels: 78.6 us -> 3.95 us  [body(): pl.pallas_call(place_kernel, grid=(steps,), out_shape=shapes, in_specs=sl...]
    pallas_call x1, Pallas kernels: 59.1 us -> 57.1 us  [body(): pl.pallas_call(functools.partial(kernel, E, PN, cap), out_shape=shapes, i...]
where the time goes in v3:
time: 61.9 us; the launch traced here: 61.7 us
  Pallas kernels  61 us (99%)
  between operations  0.64 us (1%)
    pallas_call x1, Pallas kernels, body(): pl.pallas_call(functools.partial(kernel, E, PN, cap), out_shape=shapes, i...  57.1 us
    pallas_call x1, Pallas kernels, body(): pl.pallas_call(place_kernel, grid=(steps,), out_shape=shapes, in_specs=sl...  3.95 us

profile of v3, /device:TPU:0, one launch (start us, length us, event | category | flops | bytes accessed | tf_op | source)
XLA Modules:
  0.0 61.7 jit_solution(15089117540395615990)
XLA Ops:
  0.6 57.1 %shard_map.94 = (bf16[1,2,192,192]{3,2,1,0:T(8,128)(2,1)}, bf16[1,1,768,768]{3,2,1,0:T(8,128)(2,1)}, bf16[1,1,768,768]{3,2,1,0:T(8,128)(2,1)}) custom-call(bf16[2,2,192,192]{3,2,1,0:T(8,128)(2,1)} %acts.1, bf16[2,192,192]{2,1,0:T(8,128)(2,1)} %cot.1, f32[2,2,192]{2,1,0:T(2,128)} %gates.1, s32[2,2,192]{2,1,0:T(2,128)} %owners.1, s32[2,2,192]{2,1,0:T(2,128)} %slots.1, ...), custom_call_target="tpu_custom_call" | custom-call | flops 3019898880 | bytes 4718592 | tf_op jit(solution)/shard_map/pallas_call | solution.py:421
  57.7 4.0 %shard_map.95 = (bf16[1,2,192,192]{3,2,1,0:T(8,128)(2,1)}, bf16[1,1,768,768]{3,2,1,0:T(8,128)(2,1)}, bf16[1,1,768,768]{3,2,1,0:T(8,128)(2,1)}) custom-call(bf16[1,2,192,192]{3,2,1,0:T(8,128)(2,1)} %get-tuple-element.6.a, bf16[1,1,768,768]{3,2,1,0:T(8,128)(2,1)} %get-tuple-element.7.b, bf16[1,1,768,768]{3,2,1,0:T(8,128)(2,1)} %get-tuple-element.8.c), custom_call_target="tpu_custom_call" | custom-call | bytes 4718592 | tf_op jit(solution)/shard_map/pallas_call | solution.py:438

commit v4 on v3

--- a/solution.py
+++ b/solution.py
@@ -39,7 +39,7 @@
 def kernel(
     E, PN, cap, acts, cot, gates, owners, slots, win_h, wout_h, grads, gin_h, gout_h,
     win, wout, gin, gout, placing, zs_a, zs_g, gat_a, gat_g, xn, xg, inv_s, pre_s, slope_s, hid_s, bp_s,
-    s_s, s_r, rs_s, rs_r, ret_s, ret_r, up_r, gate_s, inner_s, xn_t, hid_t, placing_t,
+    s_s, s_r, rs_s, rs_r, ret_s, ret_r, up_r, gate_s, inner_s, xn_t, hid_t, placing_t, win_t, wout_t,
     zsem_a, zrec_a, zsem_g, zrec_g, psem_a, prec_a, psem_g, prec_g,
     ssem, srec, rsem, rrec, tsem, trec, upsem, uprec, lsem, go_sem,
 ):
@@ -175,32 +175,27 @@
             u = dot(xn[rows, :], win[:, col], 1, 0)
             square = u * u
             tangent = jnp.tanh(0.7978845608 * (u + 0.044715 * square * u))
-            pre_s[rows, col] = u
+            pre_s[rows, col] = u.astype(BF)
             hid_s[rows, col] = (0.5 * u * (1.0 + tangent)).astype(BF)
             slope_s[rows, col] = 0.5 * (1.0 + tangent) + 0.5 * u * (1.0 - tangent * tangent) * 0.7978845608 * (
                 1.0 + 0.134145 * square)
 
     def backward_pass(j):
         g, rows = take(gat_g, psem_g, prec_g, j, grad_rows)
-        inner = jnp.zeros((unit, 1), F32)
+        inner = jnp.zeros((unit, tile), F32)
         for t in range(H // tile):
             col = pl.ds(t * tile, tile)
-            back = dot(xg[rows, :], wout[col, :], 1, 1)
+            back = dot(xg[rows, :], wout_t[:, col], 1, 0)
             low = (back * slope_s[rows, col]).astype(BF)
             bp_s[rows, col] = low
-            inner = inner + jnp.sum(low.astype(F32) * pre_s[rows, col], axis=1, keepdims=True)
-        inner_s[rows, :] = inner
-
-        def partial_for(q, out):
-            weights = win[pl.ds(pl.multiple_of(q * F, 16), F), :]
-            blocks = dot(bp_s[rows, :], weights, 1, 1).reshape(ge, M, cap, F)
-            joined = jnp.concatenate([blocks[:, m] for m in range(M)], axis=-1)
-            out[q, pl.ds(g * ge, ge)] = joined.astype(BF)
-
+            inner = inner + low.astype(F32) * pre_s[rows, col].astype(F32)
+        inner_s[rows, :] = jnp.sum(inner, axis=1, keepdims=True)
+        part = dot(bp_s[rows, :], win_t[...], 1, 0).reshape(ge, M, cap, D)
+        for q in range(PN):
+            joined = jnp.concatenate([part[:, m, :, q * F:(q + 1) * F] for m in range(M)], axis=-1)
+            rs_s[q, pl.ds(g * ge, ge)] = joined.astype(BF)
         for k in range(PN - 1, 0, -1):
-            q = lax.rem(mp + k, PN)
-            partial_for(q, rs_s)
-            r_copy(q, mp, g).start()
+            r_copy(lax.rem(mp + k, PN), mp, g).start()
 
         def inner_row(i):
             e = g * ge + i
@@ -211,7 +206,7 @@
         repeat(ge, inner_row)
         for k in range(1, PN):
             s_copy(lax.rem(mp + k, PN), mp, g).start()
-        partial_for(mp, rs_r)
+        rs_r[mp, pl.ds(g * ge, ge)] = rs_s[mp, pl.ds(g * ge, ge)]
 
     def turn():
         for t in range(D // 128):
@@ -296,6 +291,15 @@
         up_r[...] = cot[...]
         send_grad()
 
+    load_in.wait()
+    load_out.wait()
+    for t in range(H // 128):
+        col = pl.ds(t * 128, 128)
+        win_t[col, :] = jnp.transpose(win[:, col])
+    for t in range(D // 128):
+        col = pl.ds(t * 128, 128)
+        wout_t[col, :] = jnp.transpose(wout[:, col])
+
     @pl.when(seg == 0)
     def _():
         pl.semaphore_wait(go_sem.at[1], 1)
@@ -313,8 +317,6 @@
     def _():
         go(0)
 
-    load_in.wait()
-    load_out.wait()
     cycle(forward_pass)
 
     @pl.when(seg == 0)
@@ -377,10 +379,25 @@
         up_copy().wait_send()
 
 
-def place_kernel(a, b, c, a_out, b_out, c_out):
-    a_out[...] = a[...]
-    b_out[...] = b[...]
-    c_out[...] = c[...]
+def place_kernel(a, b, c, a_out, b_out, c_out, a_mid, b_mid, c_mid, in_sem, out_sem):
+    moves = []
+    for src, mid, dst, axis in ((a, a_mid, a_out, 1), (b, b_mid, b_out, 2), (c, c_mid, c_out, 2)):
+        cuts = src.shape[1] if axis == 1 else 4
+        step = src.shape[axis] // cuts
+        for i in range(cuts):
+            at = (slice(None),) * axis + (pl.ds(i * step, step),)
+            n = len(moves)
+            moves.append((
+                pltpu.make_async_copy(src.at[at], mid.at[at], in_sem.at[n]),
+                pltpu.make_async_copy(mid.at[at], dst.at[at], out_sem.at[n]),
+            ))
+    for first, _ in moves:
+        first.start()
+    for first, second in moves:
+        first.wait()
+        second.start()
+    for _, second in moves:
+        second.wait()
 
 
 def body(acts, cotangent, gates, owners, slots, w_in, w_out):
@@ -400,12 +417,12 @@
         vm((M, R, T), BF), vm((E, cap, W), BF), vm((E, cap, W), BF),
         vm((PN, E, cap, W), BF), vm((PN, E, cap, W), BF),
         vm((M * R, D), BF), vm((M * R, D), BF), vm((M * R, 1), F32),
-        vm((M * R, H), F32), vm((M * R, H), F32), vm((M * R, H), BF), vm((M * R, H), BF),
+        vm((M * R, H), BF), vm((M * R, H), F32), vm((M * R, H), BF), vm((M * R, H), BF),
         vm((E, 1, M * cap), F32), vm((PN, E, 1, M * cap), F32),
         vm((PN, E, cap, W), BF), vm((PN, E, cap, W), BF),
         vm((E, cap, W), BF), vm((E, cap, W), BF), vm((M, T, F), BF),
         vm((M, T, 1), F32), vm((M * R, 1), F32),
-        vm((D, M * R), BF), vm((H, M * R), BF), vm((M, T, R), BF),
+        vm((D, M * R), BF), vm((H, M * R), BF), vm((M, T, R), BF), vm((H, D), BF), vm((D, H), BF),
         dma((E,)), dma((E,)), dma((E,)), dma((E,)),
         dma((PN, groups)), dma((PN, groups)), dma((PN, groups)), dma((PN, groups)),
         dma((PN, groups)), dma((PN, groups)), dma((PN, groups)), dma((PN, groups)),
@@ -425,22 +442,16 @@
         out_specs=(whole, away, away),
         scratch_shapes=scratch,
         compiler_params=pltpu.CompilerParams(
-            collective_id=0, has_side_effects=True, vmem_limit_bytes=56 * 1024 * 1024),
+            collective_id=0, has_side_effects=True, vmem_limit_bytes=58 * 1024 * 1024),
         cost_estimate=pl.CostEstimate(
             flops=10 * M * R * D * H, bytes_accessed=8 * D * H, transcendentals=M * R * H),
     )(acts, cotangent, gates, owners, slots, w_in, w_out)
-    steps = 4
-    slices = [
-        pl.BlockSpec((1, M, T // steps, F), lambda i: (0, 0, i, 0)),
-        pl.BlockSpec((1, 1, D // steps, H), lambda i: (0, 0, i, 0)),
-        pl.BlockSpec((1, 1, H // steps, D), lambda i: (0, 0, i, 0)),
-    ]
     return pl.pallas_call(
         place_kernel,
-        grid=(steps,),
         out_shape=shapes,
-        in_specs=slices,
-        out_specs=tuple(slices),
+        in_specs=[away] * 3,
+        out_specs=(away,) * 3,
+        scratch_shapes=[vm(x.shape, BF) for x in shapes] + [dma((M + 8,)), dma((M + 8,))],
         cost_estimate=pl.CostEstimate(flops=0, bytes_accessed=8 * D * H, transcendentals=0),
     )(*held)
 

time: 61.9 us -> 54.2 us (0.88)
  Pallas kernels: 61 us -> 53.4 us
    pallas_call x1, Pallas kernels: 57.1 us -> 50.8 us  [body(): pl.pallas_call(functools.partial(kernel, E, PN, cap), out_shape=shapes, i...]
    pallas_call x1, Pallas kernels: 3.95 us -> 2.63 us  [body(): pl.pallas_call(place_kernel, out_shape=shapes, in_specs=[away] * 3, out_s...]
where the time goes in v4:
time: 54.2 us; the launch traced here: 54 us
  Pallas kernels  53.4 us (99%)
  between operations  0.64 us (1%)
    pallas_call x1, Pallas kernels, body(): pl.pallas_call(functools.partial(kernel, E, PN, cap), out_shape=shapes, i...  50.8 us
    pallas_call x1, Pallas kernels, body(): pl.pallas_call(place_kernel, out_shape=shapes, in_specs=[away] * 3, out_s...  2.63 us

profile of v4, /device:TPU:0, one launch (start us, length us, event | category | flops | bytes accessed | tf_op | source)
XLA Modules:
  0.0 54.0 jit_solution(3874308247044609039)
XLA Ops:
  0.6 50.8 %shard_map.94 = (bf16[1,2,192,192]{3,2,1,0:T(8,128)(2,1)}, bf16[1,1,768,768]{3,2,1,0:T(8,128)(2,1)}, bf16[1,1,768,768]{3,2,1,0:T(8,128)(2,1)}) custom-call(bf16[2,2,192,192]{3,2,1,0:T(8,128)(2,1)} %acts.1, bf16[2,192,192]{2,1,0:T(8,128)(2,1)} %cot.1, f32[2,2,192]{2,1,0:T(2,128)} %gates.1, s32[2,2,192]{2,1,0:T(2,128)} %owners.1, s32[2,2,192]{2,1,0:T(2,128)} %slots.1, ...), custom_call_target="tpu_custom_call" | custom-call | flops 3019898880 | bytes 4718592 | tf_op jit(solution)/shard_map/pallas_call | solution.py:438
  51.4 2.6 %shard_map.95 = (bf16[1,2,192,192]{3,2,1,0:T(8,128)(2,1)}, bf16[1,1,768,768]{3,2,1,0:T(8,128)(2,1)}, bf16[1,1,768,768]{3,2,1,0:T(8,128)(2,1)}) custom-call(bf16[1,2,192,192]{3,2,1,0:T(8,128)(2,1)} %get-tuple-element.6.a, bf16[1,1,768,768]{3,2,1,0:T(8,128)(2,1)} %get-tuple-element.7.b, bf16[1,1,768,768]{3,2,1,0:T(8,128)(2,1)} %get-tuple-element.8.c), custom_call_target="tpu_custom_call" | custom-call | bytes 4718592 | tf_op jit(solution)/shard_map/pallas_call | solution.py:449

commit v5 on v4

--- a/solution.py
+++ b/solution.py
@@ -107,8 +107,11 @@
         for k in range(PN - 1, 0, -1):
             p_copy(gat, psems, precs, lax.rem(mp + k, PN), mp, g).start()
 
+    def turn_for(j):
+        return lax.rem(mg + 2 * groups - 1 - j, groups)
+
     def gathered(gat, psems, precs, j):
-        g = lax.rem(mg + groups - j, groups)
+        g = turn_for(j)
         for k in range(1, PN):
             q = lax.rem(mp + k, PN)
             p_copy(gat, psems, precs, q, q, g).wait_recv()
@@ -232,7 +235,7 @@
             device_id={"expert": d}, device_id_type=MESH)
 
     def give_back(j):
-        g = lax.rem(mg + groups - j, groups)
+        g = turn_for(j)
         for k in range(1, PN):
             q = lax.rem(mp + k, PN)
             r_copy(q, q, g).wait_recv()
@@ -293,15 +296,16 @@
 
     load_in.wait()
     load_out.wait()
-    for t in range(H // 128):
-        col = pl.ds(t * 128, 128)
-        win_t[col, :] = jnp.transpose(win[:, col])
-    for t in range(D // 128):
-        col = pl.ds(t * 128, 128)
-        wout_t[col, :] = jnp.transpose(wout[:, col])
+
+    def turn_weights(src, dst):
+        for t in range(src.shape[1] // 128):
+            col = pl.ds(t * 128, 128)
+            dst[col, :] = jnp.transpose(src[:, col])
 
     @pl.when(seg == 0)
     def _():
+        turn_weights(win, win_t)
+        turn_weights(wout, wout_t)
         pl.semaphore_wait(go_sem.at[1], 1)
 
     def both(j):
@@ -310,6 +314,10 @@
         @pl.when(seg == 1)
         def _():
             forward(*g_set, j)
+            if j == 0:
+                turn_weights(win, win_t)
+            if j == min(1, groups - 1):
+                turn_weights(wout, wout_t)
 
     repeat(groups, both)
 
@@ -318,6 +326,10 @@
         go(0)
 
     cycle(forward_pass)
+
+    @pl.when(seg == 1)
+    def _():
+        go(1)
 
     @pl.when(seg == 0)
     def _():
@@ -326,17 +338,20 @@
         send_grad()
         repeat(groups, lambda j: forward(*g_set, j))
 
-    cycle(backward_pass)
-
-    @pl.when(seg == 1)
-    def _():
-        go(1)
+    def backward_and_back(j):
+        backward_pass(j)
+
+        @pl.when(j > 0)
+        def _():
+            give_back(j - 1)
+
+    cycle(backward_and_back)
 
     @pl.when(seg == 0)
     def _():
         first_grad()
 
-    cycle(give_back)
+    give_back(groups - 1)
     ret_r[me] = ret_s[me]
 
     @pl.when(seg == 0)

time: 54.2 us -> 59.2 us (1.092)
  Pallas kernels: 53.4 us -> 58.4 us
    pallas_call x1, Pallas kernels: 50.8 us -> 55.8 us  [body(): pl.pallas_call(functools.partial(kernel, E, PN, cap), out_shape=shapes, i...]
where the time goes in v5:
time: 59.2 us; the launch traced here: 59 us
  Pallas kernels  58.4 us (99%)
  between operations  0.64 us (1%)
    pallas_call x1, Pallas kernels, body(): pl.pallas_call(functools.partial(kernel, E, PN, cap), out_shape=shapes, i...  55.8 us
    pallas_call x1, Pallas kernels, body(): pl.pallas_call(place_kernel, out_shape=shapes, in_specs=[away] * 3, out_s...  2.63 us

profile of v5, /device:TPU:0, one launch (start us, length us, event | category | flops | bytes accessed | tf_op | source)
XLA Modules:
  0.0 59.0 jit_solution(2167185843290965819)
XLA Ops:
  0.6 55.8 %shard_map.94 = (bf16[1,2,192,192]{3,2,1,0:T(8,128)(2,1)}, bf16[1,1,768,768]{3,2,1,0:T(8,128)(2,1)}, bf16[1,1,768,768]{3,2,1,0:T(8,128)(2,1)}) custom-call(bf16[2,2,192,192]{3,2,1,0:T(8,128)(2,1)} %acts.1, bf16[2,192,192]{2,1,0:T(8,128)(2,1)} %cot.1, f32[2,2,192]{2,1,0:T(2,128)} %gates.1, s32[2,2,192]{2,1,0:T(2,128)} %owners.1, s32[2,2,192]{2,1,0:T(2,128)} %slots.1, ...), custom_call_target="tpu_custom_call" | custom-call | flops 3019898880 | bytes 4718592 | tf_op jit(solution)/shard_map/pallas_call | solution.py:453
  56.4 2.6 %shard_map.95 = (bf16[1,2,192,192]{3,2,1,0:T(8,128)(2,1)}, bf16[1,1,768,768]{3,2,1,0:T(8,128)(2,1)}, bf16[1,1,768,768]{3,2,1,0:T(8,128)(2,1)}) custom-call(bf16[1,2,192,192]{3,2,1,0:T(8,128)(2,1)} %get-tuple-element.6.a, bf16[1,1,768,768]{3,2,1,0:T(8,128)(2,1)} %get-tuple-element.7.b, bf16[1,1,768,768]{3,2,1,0:T(8,128)(2,1)} %get-tuple-element.8.c), custom_call_target="tpu_custom_call" | custom-call | bytes 4718592 | tf_op jit(solution)/shard_map/pallas_call | solution.py:464

commit v6 on v5

--- a/solution.py
+++ b/solution.py
@@ -108,7 +108,7 @@
             p_copy(gat, psems, precs, lax.rem(mp + k, PN), mp, g).start()
 
     def turn_for(j):
-        return lax.rem(mg + 2 * groups - 1 - j, groups)
+        return lax.rem(mg + groups - j, groups)
 
     def gathered(gat, psems, precs, j):
         g = turn_for(j)
@@ -327,10 +327,6 @@
 
     cycle(forward_pass)
 
-    @pl.when(seg == 1)
-    def _():
-        go(1)
-
     @pl.when(seg == 0)
     def _():
         turn()
@@ -341,11 +337,18 @@
     def backward_and_back(j):
         backward_pass(j)
 
-        @pl.when(j > 0)
+        @pl.when((seg == 1) & (j == groups // 2))
         def _():
-            give_back(j - 1)
-
+            go(1)
+
+        @pl.when(j >= lag)
+        def _():
+            give_back(j - lag)
+
+    lag = min(2, groups)
     cycle(backward_and_back)
+    if lag == 2:
+        give_back(groups - 2)
 
     @pl.when(seg == 0)
     def _():

time: 59.2 us -> 57 us (0.963)
  Pallas kernels: 58.4 us -> 56.2 us
    pallas_call x1, Pallas kernels: 55.8 us -> 53.6 us  [body(): pl.pallas_call(functools.partial(kernel, E, PN, cap), out_shape=shapes, i...]
where the time goes in v6:
time: 57 us; the launch traced here: 56.9 us
  Pallas kernels  56.2 us (99%)
  between operations  0.64 us (1%)
    pallas_call x1, Pallas kernels, body(): pl.pallas_call(functools.partial(kernel, E, PN, cap), out_shape=shapes, i...  53.6 us
    pallas_call x1, Pallas kernels, body(): pl.pallas_call(place_kernel, out_shape=shapes, in_specs=[away] * 3, out_s...  2.63 us

profile of v6, /device:TPU:0, one launch (start us, length us, event | category | flops | bytes accessed | tf_op | source)
XLA Modules:
  0.0 56.9 jit_solution(15109421401297052409)
XLA Ops:
  0.6 53.6 %shard_map.94 = (bf16[1,2,192,192]{3,2,1,0:T(8,128)(2,1)}, bf16[1,1,768,768]{3,2,1,0:T(8,128)(2,1)}, bf16[1,1,768,768]{3,2,1,0:T(8,128)(2,1)}) custom-call(bf16[2,2,192,192]{3,2,1,0:T(8,128)(2,1)} %acts.1, bf16[2,192,192]{2,1,0:T(8,128)(2,1)} %cot.1, f32[2,2,192]{2,1,0:T(2,128)} %gates.1, s32[2,2,192]{2,1,0:T(2,128)} %owners.1, s32[2,2,192]{2,1,0:T(2,128)} %slots.1, ...), custom_call_target="tpu_custom_call" | custom-call | flops 3019898880 | bytes 4718592 | tf_op jit(solution)/shard_map/pallas_call | solution.py:456
  54.2 2.6 %shard_map.95 = (bf16[1,2,192,192]{3,2,1,0:T(8,128)(2,1)}, bf16[1,1,768,768]{3,2,1,0:T(8,128)(2,1)}, bf16[1,1,768,768]{3,2,1,0:T(8,128)(2,1)}) custom-call(bf16[1,2,192,192]{3,2,1,0:T(8,128)(2,1)} %get-tuple-element.6.a, bf16[1,1,768,768]{3,2,1,0:T(8,128)(2,1)} %get-tuple-element.7.b, bf16[1,1,768,768]{3,2,1,0:T(8,128)(2,1)} %get-tuple-element.8.c), custom_call_target="tpu_custom_call" | custom-call | bytes 4718592 | tf_op jit(solution)/shard_map/pallas_call | solution.py:467

commit v7 on v4

--- a/solution.py
+++ b/solution.py
@@ -332,15 +332,12 @@
     def _():
         go(1)
 
-    @pl.when(seg == 0)
-    def _():
-        first_grad()
-
     cycle(give_back)
     ret_r[me] = ret_s[me]
 
     @pl.when(seg == 0)
     def _():
+        first_grad()
         second_grad()
 
     def back_arrive(k):

time: 54.2 us -> 54.2 us (level)
  no operation moved by 1% of the time
where the time goes in v7:
time: 54.2 us; the launch traced here: 54 us
  Pallas kernels  53.4 us (99%)
  between operations  0.64 us (1%)
    pallas_call x1, Pallas kernels, body(): pl.pallas_call(functools.partial(kernel, E, PN, cap), out_shape=shapes, i...  50.8 us
    pallas_call x1, Pallas kernels, body(): pl.pallas_call(place_kernel, out_shape=shapes, in_specs=[away] * 3, out_s...  2.63 us

profile of v7, /device:TPU:0, one launch (start us, length us, event | category | flops | bytes accessed | tf_op | source)
XLA Modules:
  0.0 54.0 jit_solution(13283260942485176285)
XLA Ops:
  0.6 50.8 %shard_map.94 = (bf16[1,2,192,192]{3,2,1,0:T(8,128)(2,1)}, bf16[1,1,768,768]{3,2,1,0:T(8,128)(2,1)}, bf16[1,1,768,768]{3,2,1,0:T(8,128)(2,1)}) custom-call(bf16[2,2,192,192]{3,2,1,0:T(8,128)(2,1)} %acts.1, bf16[2,192,192]{2,1,0:T(8,128)(2,1)} %cot.1, f32[2,2,192]{2,1,0:T(2,128)} %gates.1, s32[2,2,192]{2,1,0:T(2,128)} %owners.1, s32[2,2,192]{2,1,0:T(2,128)} %slots.1, ...), custom_call_target="tpu_custom_call" | custom-call | flops 3019898880 | bytes 4718592 | tf_op jit(solution)/shard_map/pallas_call | solution.py:435
  51.4 2.6 %shard_map.95 = (bf16[1,2,192,192]{3,2,1,0:T(8,128)(2,1)}, bf16[1,1,768,768]{3,2,1,0:T(8,128)(2,1)}, bf16[1,1,768,768]{3,2,1,0:T(8,128)(2,1)}) custom-call(bf16[1,2,192,192]{3,2,1,0:T(8,128)(2,1)} %get-tuple-element.6.a, bf16[1,1,768,768]{3,2,1,0:T(8,128)(2,1)} %get-tuple-element.7.b, bf16[1,1,768,768]{3,2,1,0:T(8,128)(2,1)} %get-tuple-element.8.c), custom_call_target="tpu_custom_call" | custom-call | bytes 4718592 | tf_op jit(solution)/shard_map/pallas_call | solution.py:446
